TPU v7x, 128 devices: a whole 4x4x4 slice. The times are simulated.
128 devices in a mesh: row: 8 (over z, y_lo), col: 16 (over x, y_hi, core).
Axes of the slice: x: 4, y: 4 (y_hi: 2, y_lo: 2; y = y_hi * 2 + y_lo), z: 4, core: 2. Of those that a mesh axis runs over, the one named last changes fastest.
Arguments:
- picture: float32 [3, 512, 2048], P(None, 'row', 'col'), may hold values from -6 to 6
- membrane: float32 [64, 256, 1024], P('row', 'col'), may hold values from -3 to 3
- dictionary: bfloat16 [1024, 3072], replicated, may hold values from -4 to 4
- momentum: float32 [1024, 3072], P(('row', 'col')), may hold values from -5 to 5
Outputs:
- final_codes: float32 [64, 256, 1024], P('row', 'col')
- new_dictionary: float32 [1024, 3072], P(('row', 'col'))
- new_momentum: float32 [1024, 3072], P(('row', 'col'))
All inputs are finite; a program needn't handle non-finite values.
Results may differ from a plain program's by a relative error of at most 0.0032.
Values may be sent and summed in bfloat16 or wider, within the bound.
A program may use at most 64 MiB of HBM per device.

v0:
```python
import jax
import jax.numpy as jnp
from jax import lax
from jax.sharding import PartitionSpec as P

PATCH_SIDE = 32
STRIDE = 8
SWEEPS = 2


THRESHOLD = 0.25
RELAXATION = 0.1
DECAY = 0.9
LEARNING = 0.25
EPSILON = 1e-05


def passed_along(block, axis, distance):
    devices = range(lax.axis_size(axis))
    route = [(i - distance, i) for i in devices if i - distance in devices]
    return lax.ppermute(block, axis, route)


def shrink(potential):
    return potential - jnp.clip(potential, -THRESHOLD, THRESHOLD)


def cells_of(picture):
    channels, height, width_px = picture.shape
    blocked = picture.reshape(channels, height // STRIDE, STRIDE, width_px // STRIDE, STRIDE)
    return blocked.transpose(1, 3, 0, 2, 4).reshape(
        height // STRIDE, width_px // STRIDE, channels * STRIDE * STRIDE
    )


def place_atoms(coding, dictionary):
    site_rows, site_cols, atom_count = coding.shape
    span_cells = PATCH_SIDE // STRIDE
    cell_size = dictionary.shape[1] // (span_cells * span_cells)
    atom_scale = dictionary.shape[1] ** (-0.5)
    placed = (
        jnp.dot(
            coding.reshape(site_rows * site_cols, atom_count),
            dictionary,
            preferred_element_type=jnp.float32,
        )
        * atom_scale
    )
    placed = placed.reshape(site_rows, site_cols, span_cells, span_cells, cell_size)
    canvas = None
    for row_off in range(span_cells):
        for col_off in range(span_cells):
            shifted = jnp.pad(
                placed[:, :, row_off, col_off],
                ((row_off, span_cells - 1 - row_off), (col_off, span_cells - 1 - col_off), (0, 0)),
            )
            canvas = shifted if canvas is None else canvas + shifted
    return canvas


def reconstruct(coding, dictionary):
    site_rows, site_cols = (coding.shape[0], coding.shape[1])
    margin = PATCH_SIDE // STRIDE - 1
    canvas = place_atoms(coding, dictionary)
    lower_spill = passed_along(canvas[site_rows:], "row", 1)
    canvas = jnp.concatenate([canvas[:margin] + lower_spill, canvas[margin:site_rows]], axis=0)
    beside = passed_along(canvas[:, site_cols:], "col", 1)
    return jnp.concatenate([canvas[:, :margin] + beside, canvas[:, margin:site_cols]], axis=1)


def extend(residual):
    margin = PATCH_SIDE // STRIDE - 1
    below_rim = passed_along(residual[:margin], "row", -1)
    tall_part = jnp.concatenate([residual, below_rim], axis=0)
    beside = passed_along(tall_part[:, :margin], "col", -1)
    return jnp.concatenate([tall_part, beside], axis=1)


def patches_of(wide_part, site_rows, site_cols):
    span_cells = PATCH_SIDE // STRIDE
    blocks = [
        wide_part[row_off : row_off + site_rows, col_off : col_off + site_cols]
        for row_off in range(span_cells)
        for col_off in range(span_cells)
    ]
    return jnp.stack(blocks, axis=2).reshape(site_rows * site_cols, -1)


def shards(picture, membrane, dictionary, momentum):
    pixels = cells_of(picture)
    site_rows, site_cols, atom_count = membrane.shape
    patch_len = dictionary.shape[1]
    atom_scale = patch_len ** (-0.5)
    potential = membrane
    for repeat in range(SWEEPS):
        active = shrink(potential)
        coding = active.astype(jnp.bfloat16)
        residual = (pixels - reconstruct(coding, dictionary)).astype(jnp.bfloat16)
        patches = patches_of(extend(residual), site_rows, site_cols)
        drive_term = (
            lax.dot_general(
                patches, dictionary, (((1,), (1,)), ((), ())), preferred_element_type=jnp.float32
            )
            * atom_scale
        )
        potential = potential + RELAXATION * (
            drive_term.reshape(site_rows, site_cols, atom_count) + active - potential
        )
    final_codes = shrink(potential)
    coding = final_codes.astype(jnp.bfloat16)
    residual = (pixels - reconstruct(coding, dictionary)).astype(jnp.bfloat16)
    wide_part = extend(residual)
    flat_codes = coding.reshape(site_rows * site_cols, atom_count)
    owned_rows = momentum.shape[0]
    final_patches = patches_of(wide_part, site_rows, site_cols)
    learning = lax.psum_scatter(
        lax.dot_general(
            flat_codes, final_patches, (((0,), (0,)), ((), ())), preferred_element_type=jnp.float32
        )
        * atom_scale,
        ("row", "col"),
        scatter_dimension=0,
        tiled=True,
    )
    owner_index = lax.axis_index(("row", "col"))
    own_atoms = lax.dynamic_slice_in_dim(
        dictionary, owner_index * owned_rows, owned_rows, 0
    ).astype(jnp.float32)
    new_momentum = DECAY * momentum + learning
    weights = own_atoms + LEARNING * new_momentum
    new_dictionary = weights * lax.rsqrt(
        jnp.mean(weights * weights, axis=1, keepdims=True) + EPSILON
    )
    return (final_codes, new_dictionary, new_momentum)


def solution(mesh):
    return jax.shard_map(
        shards,
        mesh=mesh,
        in_specs=(P(None, "row", "col"), P("row", "col", None), P(), P(("row", "col"), None)),
        out_specs=(P("row", "col", None), P(("row", "col"), None), P(("row", "col"), None)),
        check_vma=False,
    )
```

profile of v0, /device:TPU:1, one launch (start us, length us, event | category | flops | bytes accessed | tf_op | source)
XLA Modules:
  0.0 842.0 jit_solution(4187430514103718571)
XLA Ops:
  8.3 5.0 convolution_multiply_fusion.3
  13.3 3.0 reshape.176
  19.7 4.0 collective-permute-start
  25.2 5.9 collective-permute-start.1
  35.5 3.2 collective-permute-done.2
  38.8 2.4 collective-permute-start.3
  42.9 4.6 collective-permute-done.3
  56.7 7.8 stack.162
  64.5 2.9 reshape.178
  67.3 5.4 convolution_multiply_fusion.5
  73.5 2.2 convolution_multiply_fusion.2
  75.7 3.0 reshape.181
  78.8 1.9 fusion.29
  82.5 4.0 collective-permute-start.4
  88.0 4.0 collective-permute-start.5
  97.8 4.7 collective-permute-done.6
  102.7 2.2 collective-permute-start.7
  105.2 6.2 collective-permute-done.7
  113.0 5.0 stack.178
  118.0 3.0 reshape.182
  121.0 5.4 convolution_multiply_fusion.4
  128.2 2.2 convolution_multiply_fusion.1
  130.4 3.0 reshape.185
  133.4 1.9 fusion.28
  137.2 3.7 collective-permute-start.8
  142.3 3.6 collective-permute-start.9
  149.5 4.9 collective-permute-done.10
  154.5 2.2 collective-permute-start.11
  157.1 6.5 collective-permute-done.11
  165.2 3.2 stack.194
  169.5 6.4 convolution_multiply_fusion
  175.9 656.4 %reduce-scatter.2.cloned.1.call-done = f32[8,3072]{1,0:T(8,128)} async-done(((f32[1024,3072]{1,0:T(8,128)}), f32[8,3072]{1,0:T(8,128)}) %reduce-scatter.2.cloned.1.call-update) | async-done | bytes 98320 | tf_op jit(solution)/shard_map/reduce_scatter | solution.py:116
  (192 shorter events, 46.7 us)
Async XLA Ops:
  7.2 825.1 %reduce-scatter.2.cloned.1.call-start = ((), (), s32[]{:S(2)}) async-start(), calls=%async_computation.1 | async-start | bytes 12681216 | tf_op jit(solution)/shard_map/reduce_scatter | solution.py:116
  16.3 7.4 copy-start.6
  19.7 5.5 collective-permute-start
  25.2 6.9 collective-permute-start.1
  32.8 5.9 collective-permute-start.2
  38.8 8.7 %collective-permute-start.3 = (bf16[11,3,192]{2,1,0:T(4,128)(2,1)S(1)}, bf16[11,3,192]{2,1,0:T(4,128)(2,1)S(1)}, u32[]{:S(2)}, u32[]{:S(2)}) collective-permute-start(bf16[11,3,192]{2,1,0:T(4,128)(2,1)S(1)} %fusion.26), channel_id=1, source_target_pairs={{1,0},{2,1},{3,2},{4,3},{5,4},{6,5},{7,6},{8,7},{9,8},{10,9},{11,1... | collective-permute-start | bytes 38024 | tf_op jit(solution)/shard_map/ppermute | solution.py:21
  56.6 16.1 %copy-start = (f32[8,16,1024]{2,1,0:T(8,128)S(1)}, f32[8,16,1024]{2,1,0:T(8,128)}, u32[]{:S(2)}) copy-start(f32[8,16,1024]{2,1,0:T(8,128)} %param.5) | copy-start | bytes 1572868
  56.6 16.9 %slice-start = ((s8[6291456]{0:T(1024)(128)(4,1)}), s8[2097152]{0:T(1024)(128)(4,1)S(1)}, s32[]{:S(2)}) async-start(s8[6291456]{0:T(1024)(128)(4,1)} %bitcast.253), calls=%async_computation.2 | async-start | bytes 4194304
  67.3 6.2 slice-start.1
  72.7 0.8 copy-start.1
  82.5 5.5 collective-permute-start.4
  88.0 4.9 collective-permute-start.5
  95.7 6.8 collective-permute-start.6
  102.7 8.7 %collective-permute-start.7 = (bf16[11,3,192]{2,1,0:T(4,128)(2,1)S(1)}, bf16[11,3,192]{2,1,0:T(4,128)(2,1)S(1)}, u32[]{:S(2)}, u32[]{:S(2)}) collective-permute-start(bf16[11,3,192]{2,1,0:T(4,128)(2,1)S(1)} %fusion.25), channel_id=1, source_target_pairs={{1,0},{2,1},{3,2},{4,3},{5,4},{6,5},{7,6},{8,7},{9,8},{10,9},{11,1... | collective-permute-start | bytes 38024 | tf_op jit(solution)/shard_map/ppermute | solution.py:21
  118.0 10.2 %slice-start.2 = ((s8[6291456]{0:T(1024)(128)(4,1)}), s8[2097152]{0:T(1024)(128)(4,1)S(1)}, s32[]{:S(2)}) async-start(s8[6291456]{0:T(1024)(128)(4,1)} %bitcast.255), calls=%async_computation.4 | async-start | bytes 4194304
  121.0 5.4 copy-start.2
  121.0 7.2 slice-start.3
  127.5 0.7 copy-start.3
  137.2 5.1 collective-permute-start.8
  142.3 4.3 collective-permute-start.9
  147.3 7.0 collective-permute-start.10
  148.9 20.6 %copy-start.4 = (bf16[8,16,1024]{2,1,0:T(8,128)(2,1)S(1)}, bf16[8,16,1024]{2,1,0:T(8,128)(2,1)}, u32[]{:S(2)}) copy-start(bf16[8,16,1024]{2,1,0:T(8,128)(2,1)} %copy-done.3) | copy-start | bytes 786436
  154.5 9.1 %collective-permute-start.11 = (bf16[11,3,192]{2,1,0:T(4,128)(2,1)S(1)}, bf16[11,3,192]{2,1,0:T(4,128)(2,1)S(1)}, u32[]{:S(2)}, u32[]{:S(2)}) collective-permute-start(bf16[11,3,192]{2,1,0:T(4,128)(2,1)S(1)} %fusion.24), channel_id=1, source_target_pairs={{1,0},{2,1},{3,2},{4,3},{5,4},{6,5},{7,6},{8,7},{9,8},{10,9},{11,1... | collective-permute-start | bytes 38024 | tf_op jit(solution)/shard_map/ppermute | solution.py:21
  175.9 656.4 %copy-start.7 = (f32[8,3072]{1,0:T(8,128)S(1)}, f32[8,3072]{1,0:T(8,128)}, u32[]{:S(2)}) copy-start(f32[8,3072]{1,0:T(8,128)} %param.7) | copy-start | bytes 294916
  833.4 1.6 copy-start.5
Sparse Core Ops, SparseCore 0:
  176.1 656.1 reduce-scatter.1
where the time goes:
time: 856 us; the launch traced here: 842 us
  waiting for transfers between devices  690 us (81%)
  local copies, waits for them, and re-layouts  64.7 us (8%)
  starting transfers between devices  35.9 us (4%)
  matrix products  26.5 us (3%)
  between operations  15.4 us (2%)
  other arithmetic  9.49 us (1%)
    reduce_scatter x1, waiting for transfers between devices, shards(): lax.psum_scatter(lax.dot_general(flat_codes, final_patches, (((0,), (0,))...  656 us
    ppermute x12, starting transfers between devices, passed_along(): return lax.ppermute(block, axis, route)  35.9 us
    ppermute x12, waiting for transfers between devices, passed_along(): return lax.ppermute(block, axis, route)  33.6 us
    another operation x51, local copies, waits for them, and re-layouts, patches_of(): return jnp.stack(blocks, axis=2).reshape(site_rows * site_cols, -1)  30.3 us
  transfers between devices with their start and end apart: 13, of which 13 were waited for; matrix products, arithmetic and copies ran while one was open for 1% of the time, Pallas kernels for 0%

commit v1 on v0

v1 whole, which is shorter than its diff:
```python
import functools

import jax
import jax.numpy as jnp
from jax import lax
from jax.experimental import pallas as pl
from jax.experimental.pallas import tpu as pltpu
from jax.sharding import PartitionSpec as P

STRIDE = 8
SPAN = 4
MARGIN = SPAN - 1
SWEEPS = 2

THRESHOLD = 0.25
RELAXATION = 0.1
DECAY = 0.9
LEARNING = 0.25
EPSILON = 1e-05

F32 = jnp.float32
BF16 = jnp.bfloat16
MESH = pl.DeviceIdType.MESH


def shrink(potential):
    return potential - jnp.clip(potential, -THRESHOLD, THRESHOLD)


def cells_of(picture):
    channels, height, width_px = picture.shape
    blocked = picture.reshape(channels, height // STRIDE, STRIDE, width_px // STRIDE, STRIDE)
    return blocked.transpose(1, 3, 0, 2, 4).reshape(
        height // STRIDE, width_px // STRIDE, channels * STRIDE * STRIDE
    )


def peers_of(rows, cols):
    offsets = {(j, 0) for j in range(rows)} | {(0, j) for j in range(cols)}
    offsets |= {(j, k % cols) for j in range(rows) for k in (1, -1)}
    return sorted(offsets - {(0, 0)})


def kernel(
    rows, cols,
    pixels_ref, membrane_ref, dictionary_hbm, momentum_ref,
    codes_out, dictionary_out, momentum_out,
    dic, pot, coding, acc, zbuf, cbuf, ext, wide,
    down_out, side_out, down_in, side_in, diag_in,
    res_ref, edge_ref, up_in, left_in, corner_in,
    codes_t, strip_codes, strip_res, strip_edge, share_out, share_in,
    load_sem, spill_send, spill_recv, halo_send, halo_recv,
    code_send, code_recv, res_send, res_recv, rim_send, rim_recv,
    share_send, share_recv,
):
    site_rows, site_cols, cell = pixels_ref.shape
    sites, atoms = pot.shape
    patch = dic.shape[1]
    band = patch // SPAN
    pair = band // 2
    scale = patch ** (-0.5)
    share = atoms // rows
    owned = momentum_ref.shape[0]
    half = patch // 2
    me_r, me_c = lax.axis_index("row"), lax.axis_index("col")

    def at(dr, dc):
        return (lax.rem(me_r + dr % rows, rows), lax.rem(me_c + dc % cols, cols))

    def remote(src, dst, send, recv, dr, dc):
        return pltpu.make_async_remote_copy(
            src_ref=src, dst_ref=dst, send_sem=send, recv_sem=recv,
            device_id=at(dr, dc), device_id_type=MESH,
        )

    loads = [
        pltpu.make_async_copy(
            dictionary_hbm.at[:, pl.ds(d * band, band)],
            dic.at[:, pl.ds(d * band, band)],
            load_sem.at[d],
        )
        for d in range(SPAN)
    ]
    for load in loads:
        load.start()

    barrier = pltpu.get_barrier_semaphore()
    peers = peers_of(rows, cols)
    for dr, dc in peers:
        pl.semaphore_signal(barrier, inc=1, device_id=at(dr, dc), device_id_type=MESH)

    pot[...] = membrane_ref[...]
    coding[...] = shrink(membrane_ref[...]).astype(BF16)
    wide[rows * site_rows :] = jnp.zeros((MARGIN, site_cols, band), BF16)
    zbuf[...] = jnp.zeros_like(zbuf)
    cbuf[...] = jnp.zeros_like(cbuf)
    pl.semaphore_wait(barrier, len(peers))

    sub = lax.broadcasted_iota(jnp.int32, (1, 8, cell), 1)
    low = sub < 4

    def packed(tall):
        n = tall.shape[0] // 2
        split = tall.reshape(n, 2, 8, cell)
        return split[:, 0] + pltpu.roll(split[:, 1], 4, 1)

    def unpacked(tight):
        n = tight.shape[0]
        both = jnp.stack([tight, pltpu.roll(tight, 4, 1)], axis=1)
        return jnp.where(low, both.reshape(2 * n, 8, cell), 0.0)

    def reconstruct(phase):
        for d in range(SPAN):
            if phase == 0:
                loads[d].wait()
            placed = jnp.dot(
                coding[...], dic[:, d * band : (d + 1) * band], preferred_element_type=F32
            ).reshape(site_rows, site_cols, band)
            if d == 0:
                acc[0:site_rows] = placed
            else:
                acc[d : d + site_rows - 1] += placed[: site_rows - 1]
                acc[d + site_rows - 1] = placed[site_rows - 1]
        zbuf[:, 0:site_cols] = acc[:, :, :pair]
        zbuf[:, site_cols:] = jnp.zeros((site_rows + MARGIN, 8, pair), F32)
        zbuf[:, 2 : site_cols + 2] += acc[:, :, pair:]
        every = zbuf[...]
        cbuf[: site_rows + MARGIN] = every[:, :, :cell]
        cbuf[: site_rows + MARGIN, 1 : site_cols + 3] += every[:, : site_cols + 2, cell:]
        down_out[phase] = cbuf[site_rows : site_rows + MARGIN, :site_cols] * scale
        side_out[phase] = packed(cbuf[:, site_cols:] * scale)
        n = site_rows // 2
        copies = [
            remote(side_out.at[phase, pl.ds(0, n)], side_in.at[phase],
                   spill_send.at[phase, 0], spill_recv.at[phase, 0], 0, 1),
            remote(down_out.at[phase], down_in.at[phase],
                   spill_send.at[phase, 1], spill_recv.at[phase, 1], 1, 0),
            remote(side_out.at[phase, pl.ds(n, 2)], diag_in.at[phase],
                   spill_send.at[phase, 2], spill_recv.at[phase, 2], 1, 1),
        ]
        for copy in copies:
            copy.start()
        own = pixels_ref[...] - cbuf[:site_rows, :site_cols] * scale
        for copy in copies:
            copy.wait()
        from_above = jnp.where(me_r > 0, down_in[phase], 0.0)
        from_left = jnp.where(me_c > 0, unpacked(side_in[phase]), 0.0)
        from_both = jnp.where(
            jnp.logical_and(me_r > 0, me_c > 0), unpacked(diag_in[phase]), 0.0
        )
        cbuf[:site_rows, :site_cols] = own
        cbuf[:MARGIN, :site_cols] -= from_above
        cbuf[:site_rows, :8] -= from_left
        cbuf[:SPAN, :8] -= from_both
        residual = cbuf[:site_rows, :site_cols].astype(BF16)
        res_ref[phase] = residual
        left_cols = jnp.where(low, residual.astype(F32)[:, :8], 0.0)
        edge_ref[phase] = packed(left_cols).reshape(site_rows * 4, cell).astype(BF16)

    def widen(n):
        x = ext[:n]
        return jnp.concatenate(
            [x[:, k : k + site_cols] for k in range(SPAN)], axis=2
        ).astype(BF16)

    for sweep in range(SWEEPS):
        reconstruct(sweep)
        copies = [
            remote(edge_ref.at[sweep], left_in.at[sweep],
                   halo_send.at[sweep, 0], halo_recv.at[sweep, 0], 0, -1),
            remote(res_ref.at[sweep, pl.ds(0, MARGIN)], up_in.at[sweep],
                   halo_send.at[sweep, 1], halo_recv.at[sweep, 1], -1, 0),
            remote(edge_ref.at[sweep, pl.ds(0, 16)], corner_in.at[sweep],
                   halo_send.at[sweep, 2], halo_recv.at[sweep, 2], -1, -1),
        ]
        for copy in copies:
            copy.start()
        ext[:site_rows, :site_cols] = res_ref[sweep].astype(F32)
        for copy in copies:
            copy.wait()
        inside_r, inside_c = me_r < rows - 1, me_c < cols - 1
        ext[site_rows : site_rows + MARGIN, :site_cols] = jnp.where(
            inside_r, up_in[sweep].astype(F32), 0.0
        )
        beside = unpacked(left_in[sweep].astype(F32).reshape(site_rows // 2, 8, cell))
        ext[:site_rows, site_cols:] = jnp.where(inside_c, beside, 0.0)
        below = unpacked(corner_in[sweep].astype(F32).reshape(2, 8, cell))
        ext[site_rows:, site_cols:] = jnp.where(
            jnp.logical_and(inside_r, inside_c), below[:MARGIN], 0.0
        )
        wide[: site_rows + MARGIN] = widen(site_rows + MARGIN)
        last = sweep == SWEEPS - 1
        step = 256 if atoms % 256 == 0 else 128
        for first in range(0, atoms, step):
            drive = jnp.zeros((sites, step), F32)
            for d in range(SPAN):
                drive += lax.dot_general(
                    wide[d : d + site_rows].reshape(sites, band),
                    dic[first : first + step, d * band : (d + 1) * band],
                    (((1,), (1,)), ((), ())),
                    preferred_element_type=F32,
                )
            old = pot[:, first : first + step]
            new = old + RELAXATION * (drive * scale + shrink(old) - old)
            codes = shrink(new)
            coding[:, first : first + step] = codes.astype(BF16)
            if last:
                codes_out[:, first : first + step] = codes
                codes_t[first : first + step] = codes.T.astype(BF16)
            else:
                pot[:, first : first + step] = new

    def share_of(row):
        return codes_t.at[pl.ds(pl.multiple_of(row * share, share), share)]

    def place_of(row):
        return strip_codes.at[:, pl.ds(pl.multiple_of(row * sites, sites), sites)]

    code_copies = [
        remote(share_of(at(j, 0)[0]), place_of(me_r), code_send.at[j], code_recv.at[j], j, 0)
        for j in range(1, rows)
    ]
    for copy in code_copies:
        copy.start()
    place_of(me_r)[...] = share_of(me_r)[...]

    reconstruct(SWEEPS)
    rim_copies = [
        remote(edge_ref.at[SWEEPS], strip_edge.at[j], rim_send.at[j], rim_recv.at[j], j, -1)
        for j in range(rows)
    ]
    res_copies = [None] + [
        remote(res_ref.at[SWEEPS], strip_res.at[j], res_send.at[j], res_recv.at[j], j, 0)
        for j in range(1, rows)
    ]
    for j in range(rows):
        rim_copies[j].start()
        if j:
            res_copies[j].start()
    for j in range(rows):
        rim_copies[j].wait()
        if j:
            res_copies[j].wait()
        block = strip_res[j] if j else res_ref[SWEEPS]
        ext[:site_rows, :site_cols] = block.astype(F32)
        beside = unpacked(strip_edge[j].astype(F32).reshape(site_rows // 2, 8, cell))
        ext[:site_rows, site_cols:] = jnp.where(me_c < cols - 1, beside, 0.0)
        source = at(-j, 0)[0]
        wide[pl.ds(source * site_rows, site_rows)] = widen(site_rows)
    for copy in code_copies:
        copy.wait()

    tall = rows * site_rows
    for e in range(2):
        parts = [
            jnp.dot(
                strip_codes[...],
                wide[d : d + tall].reshape(tall * site_cols, band),
                preferred_element_type=F32,
            ).reshape(cols, owned, band)
            for d in (e, e + 2)
        ]
        share_out[:, :, e * band : (e + 1) * band] = jnp.concatenate(parts, axis=1).astype(BF16)
    share_copies = [
        remote(share_out.at[at(0, j)[1]], share_in.at[j], share_send.at[j], share_recv.at[j], 0, j)
        for j in range(1, cols)
    ]
    for copy in share_copies:
        copy.start()
    total = share_out[me_c].astype(F32)
    for j in range(1, cols):
        share_copies[j - 1].wait()
        total += share_in[j].astype(F32)

    for h in range(2):
        momentum_out[:, h * half : (h + 1) * half] = (
            DECAY * momentum_ref[:, h * half : (h + 1) * half]
            + total[h * owned : (h + 1) * owned] * scale
        )
    tile = 2 * owned
    index = me_r * cols + me_c
    first = pl.multiple_of(lax.div(index, 2) * tile, tile)
    both = dic[pl.ds(first, tile)].astype(F32)
    own_atoms = jnp.where(lax.rem(index, 2) == 1, both[owned:], both[:owned])
    weights = own_atoms + LEARNING * momentum_out[...]
    dictionary_out[...] = weights * lax.rsqrt(
        jnp.mean(weights * weights, axis=1, keepdims=True) + EPSILON
    )


def shards(picture, membrane, dictionary, momentum):
    pixels = cells_of(picture)
    site_rows, site_cols, atoms = membrane.shape
    sites = site_rows * site_cols
    patch = dictionary.shape[1]
    cell = pixels.shape[2]
    band, half = patch // SPAN, patch // 2
    owned = momentum.shape[0]
    rows, cols = lax.axis_size("row"), lax.axis_size("col")
    phases = SWEEPS + 1
    vmem, dma = pltpu.VMEM, pltpu.SemaphoreType.DMA
    in_vmem = pl.BlockSpec(memory_space=pltpu.VMEM)
    codes, new_dictionary, new_momentum = pl.pallas_call(
        functools.partial(kernel, rows, cols),
        out_shape=(
            jax.ShapeDtypeStruct((sites, atoms), F32),
            jax.ShapeDtypeStruct((owned, patch), F32),
            jax.ShapeDtypeStruct((owned, patch), F32),
        ),
        in_specs=[in_vmem, in_vmem, pl.BlockSpec(memory_space=pl.ANY), in_vmem],
        out_specs=(in_vmem, in_vmem, in_vmem),
        scratch_shapes=[
            vmem((atoms, patch), BF16),
            vmem((sites, atoms), F32),
            vmem((sites, atoms), BF16),
            vmem((site_rows + MARGIN, site_cols, band), F32),
            vmem((site_rows + MARGIN, site_cols + 8, band // 2), F32),
            vmem((site_rows + SPAN, site_cols + 8, cell), F32),
            vmem((site_rows + MARGIN, site_cols + 8, cell), F32),
            vmem((rows * site_rows + MARGIN, site_cols, band), BF16),
            vmem((phases, MARGIN, site_cols, cell), F32),
            vmem((phases, site_rows // 2 + 2, 8, cell), F32),
            vmem((phases, MARGIN, site_cols, cell), F32),
            vmem((phases, site_rows // 2, 8, cell), F32),
            vmem((phases, 2, 8, cell), F32),
            vmem((phases, site_rows, site_cols, cell), BF16),
            vmem((phases, site_rows * 4, cell), BF16),
            vmem((SWEEPS, MARGIN, site_cols, cell), BF16),
            vmem((SWEEPS, site_rows * 4, cell), BF16),
            vmem((SWEEPS, 16, cell), BF16),
            vmem((atoms, sites), BF16),
            vmem((atoms // rows, rows * sites), BF16),
            vmem((rows, site_rows, site_cols, cell), BF16),
            vmem((rows, site_rows * 4, cell), BF16),
            vmem((cols, 2 * owned, half), BF16),
            vmem((cols, 2 * owned, half), BF16),
            dma((SPAN,)),
            dma((phases, 3)), dma((phases, 3)),
            dma((SWEEPS, 3)), dma((SWEEPS, 3)),
            dma((rows,)), dma((rows,)),
            dma((rows,)), dma((rows,)),
            dma((rows,)), dma((rows,)),
            dma((cols,)), dma((cols,)),
        ],
        compiler_params=pltpu.CompilerParams(
            collective_id=0, has_side_effects=True, vmem_limit_bytes=48 * 2**20
        ),
    )(pixels, membrane.reshape(sites, atoms), dictionary, momentum)
    return codes.reshape(membrane.shape), new_dictionary, new_momentum


def solution(mesh):
    return jax.shard_map(
        shards,
        mesh=mesh,
        in_specs=(P(None, "row", "col"), P("row", "col", None), P(), P(("row", "col"), None)),
        out_specs=(P("row", "col", None), P(("row", "col"), None), P(("row", "col"), None)),
        check_vma=False,
    )
```

time: 856 us -> 71 us (0.08); the launches traced: 842 us -> 70.8 us
  waiting for transfers between devices: 690 us -> 0 us
  Pallas kernels: 0 us -> 63.6 us
  local copies, waits for them, and re-layouts: 64.7 us -> 6.52 us
  starting transfers between devices: 35.9 us -> 0 us
  matrix products: 26.5 us -> 0 us
  between operations: 15.4 us -> 0.65 us
  other arithmetic: 9.49 us -> 0 us
    reduce_scatter x1 -> x0, waiting for transfers between devices: 656 us -> none  [shards(): lax.psum_scatter(lax.dot_general(flat_codes, final_patches, (((0,), (0,))...]
    pallas_call x0 -> x1, Pallas kernels: none -> 63.6 us  [shards(): pl.pallas_call(functools.partial(kernel, rows, cols), out_shape=(jax.Shap...]
    ppermute x12 -> x0, starting transfers between devices: 35.9 us -> none  [passed_along(): return lax.ppermute(block, axis, route)]
    ppermute x12 -> x0, waiting for transfers between devices: 33.6 us -> none  [passed_along(): return lax.ppermute(block, axis, route)]
    another operation x51 -> x0, local copies, waits for them, and re-layouts: 30.3 us -> none  [patches_of(): return jnp.stack(blocks, axis=2).reshape(site_rows * site_cols, -1)]
    dot_general x6 -> x0, matrix products: 26.5 us -> none  [the longest x2 10.8 us: shards(): lax.dot_general(patches, dictionary, (((1,), (1,)), ((), ())), preferred_...]
    reshape x6 -> x1, local copies, waits for them, and re-layouts: 16.1 us -> 0.32 us  [cells_of(): blocked.transpose(1, 3, 0, 2, 4)]
  transfers between devices with their start and end apart: 13 -> 0, of which waited for: 13 -> 0; matrix products, arithmetic and copies ran while one was open for 1% -> 0% of each run, Pallas kernels for 0% -> 0%
where the time goes in v1:
time: 71 us; the launch traced here: 70.8 us
  Pallas kernels  63.6 us (90%)
  local copies, waits for them, and re-layouts  6.52 us (9%)
    pallas_call x1, Pallas kernels, shards(): pl.pallas_call(functools.partial(kernel, rows, cols), out_shape=(jax.Shap...  63.6 us
    unnamed x7, local copies, waits for them, and re-layouts  4.02 us
    reshape x1, local copies, waits for them, and re-layouts, cells_of(): picture.reshape(channels, height // STRIDE, STRIDE, width_px // STRIDE, S...  1.73 us

profile of v1, /device:TPU:1, one launch (start us, length us, event | category | flops | bytes accessed | tf_op | source)
XLA Modules:
  0.0 70.8 jit_solution(5529777128559205937)
XLA Ops:
  0.6 1.7 %reshape.18 = f32[3,8,8,16,8]{4,3,2,1,0:T(8,128)S(1)} reshape(f32[3,64,128]{2,1,0:T(8,128)} %param.4) | data formatting | bytes 196608 | tf_op jit(solution)/shard_map/reshape | solution.py:32
  2.4 0.5 copy.8
  2.8 0.3 copy.9.pixels_ref
  3.1 0.0 copy-start
  3.1 1.1 %copy-done = f32[8,16,1024]{2,1,0:T(8,128)S(1)} copy-done((f32[8,16,1024]{2,1,0:T(8,128)S(1)}, f32[8,16,1024]{2,1,0:T(8,128)}, u32[]{:S(2)}) %copy-start) | copy-done | bytes 524312
  4.2 0.0 copy-start.1
  4.2 0.9 %copy-done.1 = f32[8,3072]{1,0:T(8,128)S(1)} copy-done((f32[8,3072]{1,0:T(8,128)S(1)}, f32[8,3072]{1,0:T(8,128)}, u32[]{:S(2)}) %copy-start.1) | copy-done | bytes 98328
  5.1 63.6 %shard_map.67 = (f32[128,1024]{1,0:T(8,128)S(1)}, f32[8,3072]{1,0:T(8,128)S(1)}, f32[8,3072]{1,0:T(8,128)S(1)}) custom-call(f32[8,16,192]{2,1,0:T(8,128)S(1)} %copy.9.pixels_ref, f32[128,1024]{1,0:T(8,128)S(1)} %bitcast.4, bf16[1024,3072]{1,0:T(8,128)(2,1)} %dictionary_hbm.1, f32[8,3072]{1,0:T(8,128)S(1)} %copy-done.1), custom_call_target="tpu_custom_call" | custom-call | tf_op jit(solution)/shard_map/pallas_call | solution.py:303
  68.7 0.8 %copy.13 = f32[8,16,1024]{2,1,0:T(8,128)} copy(f32[8,16,1024]{2,1,0:T(8,128)S(1)} %bitcast.5) | data formatting | bytes 1048576
  69.5 0.6 copy.14
  70.1 0.6 copy.15
Async XLA Ops:
  3.1 1.1 %copy-start = (f32[8,16,1024]{2,1,0:T(8,128)S(1)}, f32[8,16,1024]{2,1,0:T(8,128)}, u32[]{:S(2)}) copy-start(f32[8,16,1024]{2,1,0:T(8,128)} %param.5) | copy-start | bytes 1572868
  4.2 0.9 %copy-start.1 = (f32[8,3072]{1,0:T(8,128)S(1)}, f32[8,3072]{1,0:T(8,128)}, u32[]{:S(2)}) copy-start(f32[8,3072]{1,0:T(8,128)} %momentum_ref.1) | copy-start | bytes 294916

commit v2 on v1

--- a/solution.py
+++ b/solution.py
@@ -43,13 +43,13 @@
 
 def kernel(
     rows, cols,
-    pixels_ref, membrane_ref, dictionary_hbm, momentum_ref,
+    pixels_ref, membrane_hbm, dictionary_hbm, momentum_hbm,
     codes_out, dictionary_out, momentum_out,
     dic, pot, coding, acc, zbuf, cbuf, ext, wide,
-    down_out, side_out, down_in, side_in, diag_in,
-    res_ref, edge_ref, up_in, left_in, corner_in,
+    down_out, up_out, t_out, l_out, above_in, below_in, left_in, right_in, corner_in,
+    res_ref, edge_ref,
     codes_t, strip_codes, strip_res, strip_edge, share_out, share_in,
-    load_sem, spill_send, spill_recv, halo_send, halo_recv,
+    momentum_ref, load_sem, spill_send, spill_recv,
     code_send, code_recv, res_send, res_recv, rim_send, rim_recv,
     share_send, share_recv,
 ):
@@ -81,7 +81,9 @@
         )
         for d in range(SPAN)
     ]
-    for load in loads:
+    membrane_load = pltpu.make_async_copy(membrane_hbm, pot, load_sem.at[SPAN])
+    momentum_load = pltpu.make_async_copy(momentum_hbm, momentum_ref, load_sem.at[SPAN + 1])
+    for load in [membrane_load] + loads + [momentum_load]:
         load.start()
 
     barrier = pltpu.get_barrier_semaphore()
@@ -89,12 +91,17 @@
     for dr, dc in peers:
         pl.semaphore_signal(barrier, inc=1, device_id=at(dr, dc), device_id_type=MESH)
 
-    pot[...] = membrane_ref[...]
-    coding[...] = shrink(membrane_ref[...]).astype(BF16)
     wide[rows * site_rows :] = jnp.zeros((MARGIN, site_cols, band), BF16)
     zbuf[...] = jnp.zeros_like(zbuf)
     cbuf[...] = jnp.zeros_like(cbuf)
-    pl.semaphore_wait(barrier, len(peers))
+    membrane_load.wait()
+    coding[...] = shrink(pot[...]).astype(BF16)
+    sent = []
+
+    def send(copies):
+        for copy in copies:
+            copy.start()
+        sent.extend(copies)
 
     sub = lax.broadcasted_iota(jnp.int32, (1, 8, cell), 1)
     low = sub < 4
@@ -127,35 +134,87 @@
         every = zbuf[...]
         cbuf[: site_rows + MARGIN] = every[:, :, :cell]
         cbuf[: site_rows + MARGIN, 1 : site_cols + 3] += every[:, : site_cols + 2, cell:]
-        down_out[phase] = cbuf[site_rows : site_rows + MARGIN, :site_cols] * scale
-        side_out[phase] = packed(cbuf[:, site_cols:] * scale)
-        n = site_rows // 2
-        copies = [
-            remote(side_out.at[phase, pl.ds(0, n)], side_in.at[phase],
-                   spill_send.at[phase, 0], spill_recv.at[phase, 0], 0, 1),
-            remote(down_out.at[phase], down_in.at[phase],
-                   spill_send.at[phase, 1], spill_recv.at[phase, 1], 1, 0),
-            remote(side_out.at[phase, pl.ds(n, 2)], diag_in.at[phase],
-                   spill_send.at[phase, 2], spill_recv.at[phase, 2], 1, 1),
-        ]
+        ext[...] = cbuf[...] * -scale
+        ext[:site_rows, :site_cols] += pixels_ref[...]
+        beyond = packed(ext[:, site_cols:])
+        within = packed(jnp.where(low, ext[:, :8], 0.0))
+        tight = lambda part: part.reshape(-1, cell)
+        tail, head = slice(site_rows // 2, None), slice(0, 2)
+        last = phase == SWEEPS
+        t_out[phase] = tight(beyond).astype(BF16)
+        down_out[phase] = jnp.concatenate(
+            [tight(ext[site_rows : site_rows + MARGIN, :site_cols]), tight(beyond[tail])]
+        ).astype(BF16)
+        if not last:
+            l_out[phase] = tight(within).astype(BF16)
+            up_out[phase] = jnp.concatenate(
+                [tight(ext[:MARGIN, :site_cols]), tight(beyond[head])]
+            ).astype(BF16)
+        own_t = site_rows * 4
+        main = MARGIN * site_cols
+        corner = pl.ds(own_t, 16)
+
+        def hop(k, src, dst, dr, dc):
+            return remote(src, dst, spill_send.at[phase, k], spill_recv.at[phase, k], dr, dc)
+
+        if last:
+            copies = [
+                hop(0, t_out.at[phase, corner], corner_in.at[phase, 0], 1, 1),
+                hop(1, down_out.at[phase, pl.ds(0, main)], above_in.at[phase, pl.ds(0, main)], 1, 0),
+                hop(2, t_out.at[phase, pl.ds(0, own_t)], left_in.at[phase, pl.ds(0, own_t)], 0, 1),
+            ]
+        else:
+            copies = [
+                hop(0, t_out.at[phase, corner], corner_in.at[phase, 0], 1, 1),
+                hop(3, l_out.at[phase, pl.ds(0, 16)], corner_in.at[phase, 1], -1, -1),
+                hop(4, l_out.at[phase, corner], corner_in.at[phase, 2], 1, -1),
+                hop(5, t_out.at[phase, pl.ds(0, 16)], corner_in.at[phase, 3], -1, 1),
+                hop(1, down_out.at[phase], above_in.at[phase], 1, 0),
+                hop(6, up_out.at[phase], below_in.at[phase], -1, 0),
+                hop(2, t_out.at[phase], left_in.at[phase], 0, 1),
+                hop(7, l_out.at[phase], right_in.at[phase], 0, -1),
+            ]
+        if phase == 0:
+            pl.semaphore_wait(barrier, len(peers))
+        send(copies)
+        return copies
+
+    has_above, has_below = me_r > 0, me_r < rows - 1
+    has_left, has_right = me_c > 0, me_c < cols - 1
+
+    def loose(ref_part):
+        return unpacked(ref_part.astype(F32).reshape(-1, 8, cell))
+
+    def gather_spill(phase, copies):
+        last = phase == SWEEPS
         for copy in copies:
-            copy.start()
-        own = pixels_ref[...] - cbuf[:site_rows, :site_cols] * scale
-        for copy in copies:
-            copy.wait()
-        from_above = jnp.where(me_r > 0, down_in[phase], 0.0)
-        from_left = jnp.where(me_c > 0, unpacked(side_in[phase]), 0.0)
-        from_both = jnp.where(
-            jnp.logical_and(me_r > 0, me_c > 0), unpacked(diag_in[phase]), 0.0
-        )
-        cbuf[:site_rows, :site_cols] = own
-        cbuf[:MARGIN, :site_cols] -= from_above
-        cbuf[:site_rows, :8] -= from_left
-        cbuf[:SPAN, :8] -= from_both
-        residual = cbuf[:site_rows, :site_cols].astype(BF16)
-        res_ref[phase] = residual
-        left_cols = jnp.where(low, residual.astype(F32)[:, :8], 0.0)
-        edge_ref[phase] = packed(left_cols).reshape(site_rows * 4, cell).astype(BF16)
+            copy.wait_recv()
+        main = MARGIN * site_cols
+        own_t = site_rows * 4
+        own, far_r, far_c = slice(0, site_rows), slice(site_rows, None), slice(site_cols, None)
+        ext[:MARGIN, :site_cols] += jnp.where(
+            has_above, above_in[phase, :main].astype(F32).reshape(MARGIN, site_cols, cell), 0.0
+        )
+        reach = own_t if last else own_t + 16
+        ext[: reach // 4, :8] += jnp.where(has_left, loose(left_in[phase, :reach]), 0.0)
+        ext[:SPAN, :8] += jnp.where(
+            jnp.logical_and(has_above, has_left), loose(corner_in[phase, 0]), 0.0
+        )
+        if last:
+            return
+        ext[far_r, :8] += jnp.where(has_left, loose(corner_in[phase, 3]), 0.0)
+        side = ext[:, far_c] + loose(right_in[phase])
+        side_head = side[:SPAN] + jnp.where(
+            has_above, loose(above_in[phase, main:]) + loose(corner_in[phase, 2]), 0.0
+        )
+        side_tail = side[site_rows:] + loose(below_in[phase, main:]) + loose(corner_in[phase, 1])
+        ext[:, far_c] = jnp.where(has_right, side, 0.0)
+        ext[:SPAN, far_c] = jnp.where(has_right, side_head, 0.0)
+        ext[far_r, far_c] = jnp.where(jnp.logical_and(has_right, has_below), side_tail, 0.0)
+        under = ext[site_rows : site_rows + MARGIN, :site_cols] + below_in[phase, :main].astype(
+            F32
+        ).reshape(MARGIN, site_cols, cell)
+        ext[site_rows : site_rows + MARGIN, :site_cols] = jnp.where(has_below, under, 0.0)
 
     def widen(n):
         x = ext[:n]
@@ -164,30 +223,7 @@
         ).astype(BF16)
 
     for sweep in range(SWEEPS):
-        reconstruct(sweep)
-        copies = [
-            remote(edge_ref.at[sweep], left_in.at[sweep],
-                   halo_send.at[sweep, 0], halo_recv.at[sweep, 0], 0, -1),
-            remote(res_ref.at[sweep, pl.ds(0, MARGIN)], up_in.at[sweep],
-                   halo_send.at[sweep, 1], halo_recv.at[sweep, 1], -1, 0),
-            remote(edge_ref.at[sweep, pl.ds(0, 16)], corner_in.at[sweep],
-                   halo_send.at[sweep, 2], halo_recv.at[sweep, 2], -1, -1),
-        ]
-        for copy in copies:
-            copy.start()
-        ext[:site_rows, :site_cols] = res_ref[sweep].astype(F32)
-        for copy in copies:
-            copy.wait()
-        inside_r, inside_c = me_r < rows - 1, me_c < cols - 1
-        ext[site_rows : site_rows + MARGIN, :site_cols] = jnp.where(
-            inside_r, up_in[sweep].astype(F32), 0.0
-        )
-        beside = unpacked(left_in[sweep].astype(F32).reshape(site_rows // 2, 8, cell))
-        ext[:site_rows, site_cols:] = jnp.where(inside_c, beside, 0.0)
-        below = unpacked(corner_in[sweep].astype(F32).reshape(2, 8, cell))
-        ext[site_rows:, site_cols:] = jnp.where(
-            jnp.logical_and(inside_r, inside_c), below[:MARGIN], 0.0
-        )
+        gather_spill(sweep, reconstruct(sweep))
         wide[: site_rows + MARGIN] = widen(site_rows + MARGIN)
         last = sweep == SWEEPS - 1
         step = 256 if atoms % 256 == 0 else 128
@@ -220,35 +256,35 @@
         remote(share_of(at(j, 0)[0]), place_of(me_r), code_send.at[j], code_recv.at[j], j, 0)
         for j in range(1, rows)
     ]
-    for copy in code_copies:
-        copy.start()
+    send(code_copies)
     place_of(me_r)[...] = share_of(me_r)[...]
 
-    reconstruct(SWEEPS)
+    gather_spill(SWEEPS, reconstruct(SWEEPS))
+    residual = ext[:site_rows, :site_cols].astype(BF16)
+    res_ref[...] = residual
+    left_cols = jnp.where(low, residual.astype(F32)[:, :8], 0.0)
+    edge_ref[...] = packed(left_cols).reshape(site_rows * 4, cell).astype(BF16)
     rim_copies = [
-        remote(edge_ref.at[SWEEPS], strip_edge.at[j], rim_send.at[j], rim_recv.at[j], j, -1)
+        remote(edge_ref, strip_edge.at[j], rim_send.at[j], rim_recv.at[j], j, -1)
         for j in range(rows)
     ]
     res_copies = [None] + [
-        remote(res_ref.at[SWEEPS], strip_res.at[j], res_send.at[j], res_recv.at[j], j, 0)
+        remote(res_ref, strip_res.at[j], res_send.at[j], res_recv.at[j], j, 0)
         for j in range(1, rows)
     ]
     for j in range(rows):
-        rim_copies[j].start()
+        send([rim_copies[j]] + ([res_copies[j]] if j else []))
+    for j in range(rows):
+        rim_copies[j].wait_recv()
         if j:
-            res_copies[j].start()
-    for j in range(rows):
-        rim_copies[j].wait()
-        if j:
-            res_copies[j].wait()
-        block = strip_res[j] if j else res_ref[SWEEPS]
+            res_copies[j].wait_recv()
+        block = strip_res[j] if j else res_ref[...]
         ext[:site_rows, :site_cols] = block.astype(F32)
-        beside = unpacked(strip_edge[j].astype(F32).reshape(site_rows // 2, 8, cell))
-        ext[:site_rows, site_cols:] = jnp.where(me_c < cols - 1, beside, 0.0)
+        ext[:site_rows, site_cols:] = jnp.where(has_right, loose(strip_edge[j]), 0.0)
         source = at(-j, 0)[0]
         wide[pl.ds(source * site_rows, site_rows)] = widen(site_rows)
     for copy in code_copies:
-        copy.wait()
+        copy.wait_recv()
 
     tall = rows * site_rows
     for e in range(2):
@@ -265,13 +301,13 @@
         remote(share_out.at[at(0, j)[1]], share_in.at[j], share_send.at[j], share_recv.at[j], 0, j)
         for j in range(1, cols)
     ]
-    for copy in share_copies:
-        copy.start()
+    send(share_copies)
     total = share_out[me_c].astype(F32)
     for j in range(1, cols):
-        share_copies[j - 1].wait()
+        share_copies[j - 1].wait_recv()
         total += share_in[j].astype(F32)
 
+    momentum_load.wait()
     for h in range(2):
         momentum_out[:, h * half : (h + 1) * half] = (
             DECAY * momentum_ref[:, h * half : (h + 1) * half]
@@ -286,6 +322,8 @@
     dictionary_out[...] = weights * lax.rsqrt(
         jnp.mean(weights * weights, axis=1, keepdims=True) + EPSILON
     )
+    for copy in sent:
+        copy.wait_send()
 
 
 def shards(picture, membrane, dictionary, momentum):
@@ -299,6 +337,7 @@
     rows, cols = lax.axis_size("row"), lax.axis_size("col")
     phases = SWEEPS + 1
     vmem, dma = pltpu.VMEM, pltpu.SemaphoreType.DMA
+    anywhere = pl.BlockSpec(memory_space=pltpu.HBM)
     in_vmem = pl.BlockSpec(memory_space=pltpu.VMEM)
     codes, new_dictionary, new_momentum = pl.pallas_call(
         functools.partial(kernel, rows, cols),
@@ -307,7 +346,7 @@
             jax.ShapeDtypeStruct((owned, patch), F32),
             jax.ShapeDtypeStruct((owned, patch), F32),
         ),
-        in_specs=[in_vmem, in_vmem, pl.BlockSpec(memory_space=pl.ANY), in_vmem],
+        in_specs=[in_vmem, anywhere, anywhere, anywhere],
         out_specs=(in_vmem, in_vmem, in_vmem),
         scratch_shapes=[
             vmem((atoms, patch), BF16),
@@ -316,27 +355,28 @@
             vmem((site_rows + MARGIN, site_cols, band), F32),
             vmem((site_rows + MARGIN, site_cols + 8, band // 2), F32),
             vmem((site_rows + SPAN, site_cols + 8, cell), F32),
-            vmem((site_rows + MARGIN, site_cols + 8, cell), F32),
+            vmem((site_rows + SPAN, site_cols + 8, cell), F32),
             vmem((rows * site_rows + MARGIN, site_cols, band), BF16),
-            vmem((phases, MARGIN, site_cols, cell), F32),
-            vmem((phases, site_rows // 2 + 2, 8, cell), F32),
-            vmem((phases, MARGIN, site_cols, cell), F32),
-            vmem((phases, site_rows // 2, 8, cell), F32),
-            vmem((phases, 2, 8, cell), F32),
-            vmem((phases, site_rows, site_cols, cell), BF16),
-            vmem((phases, site_rows * 4, cell), BF16),
-            vmem((SWEEPS, MARGIN, site_cols, cell), BF16),
-            vmem((SWEEPS, site_rows * 4, cell), BF16),
-            vmem((SWEEPS, 16, cell), BF16),
+            vmem((phases, MARGIN * site_cols + 16, cell), BF16),
+            vmem((phases, MARGIN * site_cols + 16, cell), BF16),
+            vmem((phases, (site_rows + SPAN) * 4, cell), BF16),
+            vmem((phases, (site_rows + SPAN) * 4, cell), BF16),
+            vmem((phases, MARGIN * site_cols + 16, cell), BF16),
+            vmem((phases, MARGIN * site_cols + 16, cell), BF16),
+            vmem((phases, (site_rows + SPAN) * 4, cell), BF16),
+            vmem((phases, (site_rows + SPAN) * 4, cell), BF16),
+            vmem((phases, 4, 16, cell), BF16),
+            vmem((site_rows, site_cols, cell), BF16),
+            vmem((site_rows * 4, cell), BF16),
             vmem((atoms, sites), BF16),
             vmem((atoms // rows, rows * sites), BF16),
             vmem((rows, site_rows, site_cols, cell), BF16),
             vmem((rows, site_rows * 4, cell), BF16),
             vmem((cols, 2 * owned, half), BF16),
             vmem((cols, 2 * owned, half), BF16),
-            dma((SPAN,)),
-            dma((phases, 3)), dma((phases, 3)),
-            dma((SWEEPS, 3)), dma((SWEEPS, 3)),
+            vmem((owned, patch), F32),
+            dma((SPAN + 2,)),
+            dma((phases, 8)), dma((phases, 8)),
             dma((rows,)), dma((rows,)),
             dma((rows,)), dma((rows,)),
             dma((rows,)), dma((rows,)),

time: 71 us -> 62.7 us (0.88)
  Pallas kernels: 63.6 us -> 55.4 us
    pallas_call x1, Pallas kernels: 63.6 us -> 55.4 us  [shards(): pl.pallas_call(functools.partial(kernel, rows, cols), out_shape=(jax.Shap...]
where the time goes in v2:
time: 62.7 us; the launch traced here: 62.5 us
  Pallas kernels  55.4 us (88%)
  local copies, waits for them, and re-layouts  6.52 us (10%)
  between operations  0.65 us (1%)
    pallas_call x1, Pallas kernels, shards(): pl.pallas_call(functools.partial(kernel, rows, cols), out_shape=(jax.Shap...  55.4 us
    unnamed x7, local copies, waits for them, and re-layouts  4.02 us
    reshape x1, local copies, waits for them, and re-layouts, cells_of(): picture.reshape(channels, height // STRIDE, STRIDE, width_px // STRIDE, S...  1.73 us

profile of v2, /device:TPU:1, one launch (start us, length us, event | category | flops | bytes accessed | tf_op | source)
XLA Modules:
  0.0 62.5 jit_solution(8182841999967833786)
XLA Ops:
  0.6 1.7 %reshape.18 = f32[3,8,8,16,8]{4,3,2,1,0:T(8,128)S(1)} reshape(f32[3,64,128]{2,1,0:T(8,128)} %param.4) | data formatting | bytes 196608 | tf_op jit(solution)/shard_map/reshape | solution.py:32
  2.4 0.5 copy.8
  2.8 0.3 copy.9.pixels_ref
  3.1 0.0 copy-start
  3.1 1.1 %copy-done = f32[8,16,1024]{2,1,0:T(8,128)S(1)} copy-done((f32[8,16,1024]{2,1,0:T(8,128)S(1)}, f32[8,16,1024]{2,1,0:T(8,128)}, u32[]{:S(2)}) %copy-start) | copy-done | bytes 524312
  4.2 0.0 copy-start.1
  4.2 0.9 %copy-done.1 = f32[8,3072]{1,0:T(8,128)S(1)} copy-done((f32[8,3072]{1,0:T(8,128)S(1)}, f32[8,3072]{1,0:T(8,128)}, u32[]{:S(2)}) %copy-start.1) | copy-done | bytes 98328
  5.1 55.4 %shard_map.67 = (f32[128,1024]{1,0:T(8,128)S(1)}, f32[8,3072]{1,0:T(8,128)S(1)}, f32[8,3072]{1,0:T(8,128)S(1)}) custom-call(f32[8,16,192]{2,1,0:T(8,128)S(1)} %copy.9.pixels_ref, f32[128,1024]{1,0:T(8,128)S(1)} %bitcast.4, bf16[1024,3072]{1,0:T(8,128)(2,1)} %dictionary_hbm.1, f32[8,3072]{1,0:T(8,128)S(1)} %copy-done.1), custom_call_target="tpu_custom_call" | custom-call | tf_op jit(solution)/shard_map/pallas_call | solution.py:342
  60.4 0.8 %copy.13 = f32[8,16,1024]{2,1,0:T(8,128)} copy(f32[8,16,1024]{2,1,0:T(8,128)S(1)} %bitcast.5) | data formatting | bytes 1048576
  61.2 0.6 %copy.14 = f32[8,3072]{1,0:T(8,128)} copy(f32[8,3072]{1,0:T(8,128)S(1)} %get-tuple-element.13) | data formatting | bytes 196608
  61.9 0.6 %copy.15 = f32[8,3072]{1,0:T(8,128)} copy(f32[8,3072]{1,0:T(8,128)S(1)} %get-tuple-element.14) | data formatting | bytes 196608
Async XLA Ops:
  3.1 1.1 %copy-start = (f32[8,16,1024]{2,1,0:T(8,128)S(1)}, f32[8,16,1024]{2,1,0:T(8,128)}, u32[]{:S(2)}) copy-start(f32[8,16,1024]{2,1,0:T(8,128)} %param.5) | copy-start | bytes 1572868
  4.2 0.9 %copy-start.1 = (f32[8,3072]{1,0:T(8,128)S(1)}, f32[8,3072]{1,0:T(8,128)}, u32[]{:S(2)}) copy-start(f32[8,3072]{1,0:T(8,128)} %momentum_hbm.1) | copy-start | bytes 294916

commit v3 on v2

--- a/solution.py
+++ b/solution.py
@@ -28,11 +28,36 @@
 
 
 def cells_of(picture):
-    channels, height, width_px = picture.shape
-    blocked = picture.reshape(channels, height // STRIDE, STRIDE, width_px // STRIDE, STRIDE)
-    return blocked.transpose(1, 3, 0, 2, 4).reshape(
-        height // STRIDE, width_px // STRIDE, channels * STRIDE * STRIDE
+    channels = picture.shape[0]
+    x = picture.reshape(-1, STRIDE, 128)
+    y_at = lax.broadcasted_iota(jnp.int32, (1, STRIDE, 128), 1)
+    lane = lax.broadcasted_iota(jnp.int32, (1, STRIDE, 128), 2)
+    for bit in (1, 2, 4):
+        from_later = pltpu.roll(pltpu.roll(x, STRIDE - bit, 1), STRIDE * bit, 2)
+        from_earlier = pltpu.roll(pltpu.roll(x, bit, 1), 128 - STRIDE * bit, 2)
+        y_bit = (y_at & bit) != 0
+        g_bit = (lane & (STRIDE * bit)) != 0
+        x = jnp.where(y_bit == g_bit, x, jnp.where(g_bit, from_later, from_earlier))
+    x = x.reshape(channels, -1, STRIDE, 128)
+    turned = pltpu.roll(x.reshape(-1, STRIDE, 128), 64, 2).reshape(x.shape)
+    lower = lane < 64
+    left = jnp.concatenate(
+        [jnp.where(lower, x[0], turned[1]), jnp.where(lower, turned[0], x[1])], axis=1
     )
+    right = jnp.concatenate([x[2], turned[2]], axis=1)
+    return jnp.concatenate([left, right[:, :, :64]], axis=2)
+
+
+def tightened(x):
+    n = x.shape[0] // 2
+    ends = jnp.concatenate([x[:n, :, 128:], x[n:, :, 128:]], axis=2)
+    return jnp.concatenate([x[:, :, :128], ends], axis=0)
+
+
+def untightened(t):
+    n = t.shape[0] * 2 // 3
+    ends = jnp.concatenate([t[n:, :, :64], t[n:, :, 64:]], axis=0)
+    return jnp.concatenate([t[:n], ends], axis=2)
 
 
 def peers_of(rows, cols):
@@ -43,9 +68,9 @@
 
 def kernel(
     rows, cols,
-    pixels_ref, membrane_hbm, dictionary_hbm, momentum_hbm,
+    picture_ref, membrane_hbm, dictionary_hbm, momentum_hbm,
     codes_out, dictionary_out, momentum_out,
-    dic, pot, coding, acc, zbuf, cbuf, ext, wide,
+    dic, dic_t, pot, coding, cells_ref, acc, zbuf, cbuf, ext, wide,
     down_out, up_out, t_out, l_out, above_in, below_in, left_in, right_in, corner_in,
     res_ref, edge_ref,
     codes_t, strip_codes, strip_res, strip_edge, share_out, share_in,
@@ -53,7 +78,7 @@
     code_send, code_recv, res_send, res_recv, rim_send, rim_recv,
     share_send, share_recv,
 ):
-    site_rows, site_cols, cell = pixels_ref.shape
+    site_rows, site_cols, cell = cells_ref.shape
     sites, atoms = pot.shape
     patch = dic.shape[1]
     band = patch // SPAN
@@ -94,6 +119,7 @@
     wide[rows * site_rows :] = jnp.zeros((MARGIN, site_cols, band), BF16)
     zbuf[...] = jnp.zeros_like(zbuf)
     cbuf[...] = jnp.zeros_like(cbuf)
+    cells_ref[...] = cells_of(picture_ref[...])
     membrane_load.wait()
     coding[...] = shrink(pot[...]).astype(BF16)
     sent = []
@@ -135,7 +161,7 @@
         cbuf[: site_rows + MARGIN] = every[:, :, :cell]
         cbuf[: site_rows + MARGIN, 1 : site_cols + 3] += every[:, : site_cols + 2, cell:]
         ext[...] = cbuf[...] * -scale
-        ext[:site_rows, :site_cols] += pixels_ref[...]
+        ext[:site_rows, :site_cols] += cells_ref[...]
         beyond = packed(ext[:, site_cols:])
         within = packed(jnp.where(low, ext[:, :8], 0.0))
         tight = lambda part: part.reshape(-1, cell)
@@ -177,6 +203,12 @@
         if phase == 0:
             pl.semaphore_wait(barrier, len(peers))
         send(copies)
+        if phase == 0:
+            for first in range(0, atoms, 256):
+                for d in range(SPAN):
+                    dic_t[d * band : (d + 1) * band, first : first + 256] = dic[
+                        first : first + 256, d * band : (d + 1) * band
+                    ].T
         return copies
 
     has_above, has_below = me_r > 0, me_r < rows - 1
@@ -230,10 +262,9 @@
         for first in range(0, atoms, step):
             drive = jnp.zeros((sites, step), F32)
             for d in range(SPAN):
-                drive += lax.dot_general(
+                drive += jnp.dot(
                     wide[d : d + site_rows].reshape(sites, band),
-                    dic[first : first + step, d * band : (d + 1) * band],
-                    (((1,), (1,)), ((), ())),
+                    dic_t[d * band : (d + 1) * band, first : first + step],
                     preferred_element_type=F32,
                 )
             old = pot[:, first : first + step]
@@ -260,10 +291,10 @@
     place_of(me_r)[...] = share_of(me_r)[...]
 
     gather_spill(SWEEPS, reconstruct(SWEEPS))
-    residual = ext[:site_rows, :site_cols].astype(BF16)
-    res_ref[...] = residual
-    left_cols = jnp.where(low, residual.astype(F32)[:, :8], 0.0)
-    edge_ref[...] = packed(left_cols).reshape(site_rows * 4, cell).astype(BF16)
+    residual = ext[:site_rows, :site_cols].astype(BF16).astype(F32)
+    res_ref[...] = tightened(residual).astype(BF16)
+    left_cols = packed(jnp.where(low, residual[:, :8], 0.0))
+    edge_ref[...] = tightened(left_cols).reshape(-1, 128).astype(BF16)
     rim_copies = [
         remote(edge_ref, strip_edge.at[j], rim_send.at[j], rim_recv.at[j], j, -1)
         for j in range(rows)
@@ -279,8 +310,8 @@
         if j:
             res_copies[j].wait_recv()
         block = strip_res[j] if j else res_ref[...]
-        ext[:site_rows, :site_cols] = block.astype(F32)
-        ext[:site_rows, site_cols:] = jnp.where(has_right, loose(strip_edge[j]), 0.0)
+        ext[:site_rows, :site_cols] = untightened(block.astype(F32))
+        ext[:site_rows, site_cols:] = jnp.where(has_right, unpacked(untightened(strip_edge[j].astype(F32).reshape(-1, 8, 128))), 0.0)
         source = at(-j, 0)[0]
         wide[pl.ds(source * site_rows, site_rows)] = widen(site_rows)
     for copy in code_copies:
@@ -327,11 +358,10 @@
 
 
 def shards(picture, membrane, dictionary, momentum):
-    pixels = cells_of(picture)
     site_rows, site_cols, atoms = membrane.shape
     sites = site_rows * site_cols
     patch = dictionary.shape[1]
-    cell = pixels.shape[2]
+    cell = patch // SPAN // SPAN
     band, half = patch // SPAN, patch // 2
     owned = momentum.shape[0]
     rows, cols = lax.axis_size("row"), lax.axis_size("col")
@@ -350,8 +380,10 @@
         out_specs=(in_vmem, in_vmem, in_vmem),
         scratch_shapes=[
             vmem((atoms, patch), BF16),
+            vmem((patch, atoms), BF16),
             vmem((sites, atoms), F32),
             vmem((sites, atoms), BF16),
+            vmem((site_rows, site_cols, cell), F32),
             vmem((site_rows + MARGIN, site_cols, band), F32),
             vmem((site_rows + MARGIN, site_cols + 8, band // 2), F32),
             vmem((site_rows + SPAN, site_cols + 8, cell), F32),
@@ -366,12 +398,12 @@
             vmem((phases, (site_rows + SPAN) * 4, cell), BF16),
             vmem((phases, (site_rows + SPAN) * 4, cell), BF16),
             vmem((phases, 4, 16, cell), BF16),
-            vmem((site_rows, site_cols, cell), BF16),
-            vmem((site_rows * 4, cell), BF16),
+            vmem((site_rows * 3 // 2, site_cols, 128), BF16),
+            vmem((site_rows * 6, 128), BF16),
             vmem((atoms, sites), BF16),
             vmem((atoms // rows, rows * sites), BF16),
-            vmem((rows, site_rows, site_cols, cell), BF16),
-            vmem((rows, site_rows * 4, cell), BF16),
+            vmem((rows, site_rows * 3 // 2, site_cols, 128), BF16),
+            vmem((rows, site_rows * 6, 128), BF16),
             vmem((cols, 2 * owned, half), BF16),
             vmem((cols, 2 * owned, half), BF16),
             vmem((owned, patch), F32),
@@ -385,7 +417,7 @@
         compiler_params=pltpu.CompilerParams(
             collective_id=0, has_side_effects=True, vmem_limit_bytes=48 * 2**20
         ),
-    )(pixels, membrane.reshape(sites, atoms), dictionary, momentum)
+    )(picture, membrane.reshape(sites, atoms), dictionary, momentum)
     return codes.reshape(membrane.shape), new_dictionary, new_momentum
 
 

time: 62.7 us -> 58 us (0.925)
  Pallas kernels: 55.4 us -> 52.3 us
  local copies, waits for them, and re-layouts: 6.52 us -> 4.89 us
    pallas_call x1, Pallas kernels: 55.4 us -> 52.3 us  [shards(): pl.pallas_call(functools.partial(kernel, rows, cols), out_shape=(jax.Shap...]
    reshape x2 -> x0, local copies, waits for them, and re-layouts: 2.05 us -> none  [the longest x1 1.73 us: cells_of(): picture.reshape(channels, height // STRIDE, STRIDE, width_px // STRIDE, S...]
    unnamed x7 -> x9, local copies, waits for them, and re-layouts: 4.02 us -> 4.89 us
where the time goes in v3:
time: 58 us; the launch traced here: 57.8 us
  Pallas kernels  52.3 us (90%)
  local copies, waits for them, and re-layouts  4.89 us (8%)
  between operations  0.65 us (1%)
    pallas_call x1, Pallas kernels, shards(): pl.pallas_call(functools.partial(kernel, rows, cols), out_shape=(jax.Shap...  52.3 us
    unnamed x9, local copies, waits for them, and re-layouts  4.89 us

profile of v3, /device:TPU:1, one launch (start us, length us, event | category | flops | bytes accessed | tf_op | source)
XLA Modules:
  0.0 57.8 jit_solution(6554811037171998284)
XLA Ops:
  0.6 0.0 copy-start
  0.6 1.0 %copy-done = f32[8,16,1024]{2,1,0:T(8,128)S(1)} copy-done((f32[8,16,1024]{2,1,0:T(8,128)S(1)}, f32[8,16,1024]{2,1,0:T(8,128)}, u32[]{:S(2)}) %copy-start) | copy-done | bytes 524312
  1.7 0.0 copy-start.1
  1.7 0.9 %copy-done.1 = f32[3,64,128]{2,1,0:T(8,128)S(1)} copy-done((f32[3,64,128]{2,1,0:T(8,128)S(1)}, f32[3,64,128]{2,1,0:T(8,128)}, u32[]{:S(2)}) %copy-start.1) | copy-done | bytes 98328
  2.6 0.0 copy-start.2
  2.6 0.9 %copy-done.2 = f32[8,3072]{1,0:T(8,128)S(1)} copy-done((f32[8,3072]{1,0:T(8,128)S(1)}, f32[8,3072]{1,0:T(8,128)}, u32[]{:S(2)}) %copy-start.2) | copy-done | bytes 98328
  3.5 52.3 %shard_map.67 = (f32[128,1024]{1,0:T(8,128)S(1)}, f32[8,3072]{1,0:T(8,128)S(1)}, f32[8,3072]{1,0:T(8,128)S(1)}) custom-call(f32[3,64,128]{2,1,0:T(8,128)S(1)} %copy-done.1, f32[128,1024]{1,0:T(8,128)S(1)} %bitcast.3, bf16[1024,3072]{1,0:T(8,128)(2,1)} %dictionary_hbm.1, f32[8,3072]{1,0:T(8,128)S(1)} %copy-done.2), custom_call_target="tpu_custom_call" | custom-call | tf_op jit(solution)/shard_map/pallas_call | solution.py:372
  55.7 0.8 %copy.10 = f32[8,16,1024]{2,1,0:T(8,128)} copy(f32[8,16,1024]{2,1,0:T(8,128)S(1)} %bitcast.2) | data formatting | bytes 1048576
  56.5 0.6 %copy.11 = f32[8,3072]{1,0:T(8,128)} copy(f32[8,3072]{1,0:T(8,128)S(1)} %get-tuple-element.13) | data formatting | bytes 196608
  57.2 0.6 %copy.12 = f32[8,3072]{1,0:T(8,128)} copy(f32[8,3072]{1,0:T(8,128)S(1)} %get-tuple-element.14) | data formatting | bytes 196608
Async XLA Ops:
  0.6 1.0 %copy-start = (f32[8,16,1024]{2,1,0:T(8,128)S(1)}, f32[8,16,1024]{2,1,0:T(8,128)}, u32[]{:S(2)}) copy-start(f32[8,16,1024]{2,1,0:T(8,128)} %param.5) | copy-start | bytes 1572868
  1.7 0.9 %copy-start.1 = (f32[3,64,128]{2,1,0:T(8,128)S(1)}, f32[3,64,128]{2,1,0:T(8,128)}, u32[]{:S(2)}) copy-start(f32[3,64,128]{2,1,0:T(8,128)} %picture_ref.1) | copy-start | bytes 294916
  2.6 0.9 %copy-start.2 = (f32[8,3072]{1,0:T(8,128)S(1)}, f32[8,3072]{1,0:T(8,128)}, u32[]{:S(2)}) copy-start(f32[8,3072]{1,0:T(8,128)} %momentum_hbm.1) | copy-start | bytes 294916

commit v4 on v3

--- a/solution.py
+++ b/solution.py
@@ -61,7 +61,7 @@
 
 
 def peers_of(rows, cols):
-    offsets = {(j, 0) for j in range(rows)} | {(0, j) for j in range(cols)}
+    offsets = {(j, 0) for j in range(rows)} | {(0, j) for j in range(0, cols, 2)}
     offsets |= {(j, k % cols) for j in range(rows) for k in (1, -1)}
     return sorted(offsets - {(0, 0)})
 
@@ -73,10 +73,10 @@
     dic, dic_t, pot, coding, cells_ref, acc, zbuf, cbuf, ext, wide,
     down_out, up_out, t_out, l_out, above_in, below_in, left_in, right_in, corner_in,
     res_ref, edge_ref,
-    codes_t, strip_codes, strip_res, strip_edge, share_out, share_in,
+    codes_t, strip_codes, strip_res, strip_edge, share_out, pair_in, summed, share_in,
     momentum_ref, load_sem, spill_send, spill_recv,
     code_send, code_recv, res_send, res_recv, rim_send, rim_recv,
-    share_send, share_recv,
+    pair_send, pair_recv, share_send, share_recv,
 ):
     site_rows, site_cols, cell = cells_ref.shape
     sites, atoms = pot.shape
@@ -86,7 +86,6 @@
     scale = patch ** (-0.5)
     share = atoms // rows
     owned = momentum_ref.shape[0]
-    half = patch // 2
     me_r, me_c = lax.axis_index("row"), lax.axis_index("col")
 
     def at(dr, dc):
@@ -142,7 +141,7 @@
         both = jnp.stack([tight, pltpu.roll(tight, 4, 1)], axis=1)
         return jnp.where(low, both.reshape(2 * n, 8, cell), 0.0)
 
-    def reconstruct(phase):
+    def reconstruct(phase, meanwhile):
         for d in range(SPAN):
             if phase == 0:
                 loads[d].wait()
@@ -203,12 +202,7 @@
         if phase == 0:
             pl.semaphore_wait(barrier, len(peers))
         send(copies)
-        if phase == 0:
-            for first in range(0, atoms, 256):
-                for d in range(SPAN):
-                    dic_t[d * band : (d + 1) * band, first : first + 256] = dic[
-                        first : first + 256, d * band : (d + 1) * band
-                    ].T
+        meanwhile()
         return copies
 
     has_above, has_below = me_r > 0, me_r < rows - 1
@@ -254,8 +248,16 @@
             [x[:, k : k + site_cols] for k in range(SPAN)], axis=2
         ).astype(BF16)
 
+    def turn_dictionary():
+        for first in range(0, atoms, 256):
+            for d in range(SPAN):
+                dic_t[d * band : (d + 1) * band, first : first + 256] = dic[
+                    first : first + 256, d * band : (d + 1) * band
+                ].T
+
     for sweep in range(SWEEPS):
-        gather_spill(sweep, reconstruct(sweep))
+        meanwhile = turn_dictionary if sweep == 0 else lambda: None
+        gather_spill(sweep, reconstruct(sweep, meanwhile))
         wide[: site_rows + MARGIN] = widen(site_rows + MARGIN)
         last = sweep == SWEEPS - 1
         step = 256 if atoms % 256 == 0 else 128
@@ -273,7 +275,6 @@
             coding[:, first : first + step] = codes.astype(BF16)
             if last:
                 codes_out[:, first : first + step] = codes
-                codes_t[first : first + step] = codes.T.astype(BF16)
             else:
                 pot[:, first : first + step] = new
 
@@ -287,10 +288,13 @@
         remote(share_of(at(j, 0)[0]), place_of(me_r), code_send.at[j], code_recv.at[j], j, 0)
         for j in range(1, rows)
     ]
-    send(code_copies)
-    place_of(me_r)[...] = share_of(me_r)[...]
-
-    gather_spill(SWEEPS, reconstruct(SWEEPS))
+
+    def give_codes():
+        codes_t[...] = codes_out[...].T.astype(BF16)
+        send(code_copies)
+        place_of(me_r)[...] = share_of(me_r)[...]
+
+    gather_spill(SWEEPS, reconstruct(SWEEPS, give_codes))
     residual = ext[:site_rows, :site_cols].astype(BF16).astype(F32)
     res_ref[...] = tightened(residual).astype(BF16)
     left_cols = packed(jnp.where(low, residual[:, :8], 0.0))
@@ -318,32 +322,49 @@
         copy.wait_recv()
 
     tall = rows * site_rows
+    core = lax.rem(me_c, 2)
+    chip = lax.div(me_c, 2)
+    chips = cols // 2
+    twin = (me_r, me_c + 1 - 2 * core)
+    pair_copies, share_copies = [], []
     for e in range(2):
         parts = [
             jnp.dot(
                 strip_codes[...],
                 wide[d : d + tall].reshape(tall * site_cols, band),
                 preferred_element_type=F32,
-            ).reshape(cols, owned, band)
+            ).reshape(chips, 2, owned, band)
             for d in (e, e + 2)
         ]
-        share_out[:, :, e * band : (e + 1) * band] = jnp.concatenate(parts, axis=1).astype(BF16)
-    share_copies = [
-        remote(share_out.at[at(0, j)[1]], share_in.at[j], share_send.at[j], share_recv.at[j], 0, j)
-        for j in range(1, cols)
-    ]
-    send(share_copies)
-    total = share_out[me_c].astype(F32)
-    for j in range(1, cols):
-        share_copies[j - 1].wait_recv()
-        total += share_in[j].astype(F32)
-
+        share_out[e] = jnp.concatenate(parts, axis=2).astype(BF16)
+        pair_copies.append(
+            pltpu.make_async_remote_copy(
+                src_ref=share_out.at[e, :, 1 - core], dst_ref=pair_in.at[e],
+                send_sem=pair_send.at[e], recv_sem=pair_recv.at[e],
+                device_id=twin, device_id_type=MESH,
+            )
+        )
+        send(pair_copies[e:])
+    for e in range(2):
+        pair_copies[e].wait_recv()
+        summed[e] = (share_out[e, :, core].astype(F32) + pair_in[e].astype(F32)).astype(BF16)
+        share_copies.append([
+            remote(summed.at[e, lax.rem(chip + j, chips)], share_in.at[e, j],
+                   share_send.at[e, j], share_recv.at[e, j], 0, 2 * j)
+            for j in range(1, chips)
+        ])
+        send(share_copies[e])
     momentum_load.wait()
-    for h in range(2):
-        momentum_out[:, h * half : (h + 1) * half] = (
-            DECAY * momentum_ref[:, h * half : (h + 1) * half]
-            + total[h * owned : (h + 1) * owned] * scale
-        )
+    for e in range(2):
+        total = summed[e, chip].astype(F32)
+        for j in range(1, chips):
+            share_copies[e][j - 1].wait_recv()
+            total += share_in[e, j].astype(F32)
+        for k in range(2):
+            span = pl.ds((e + 2 * k) * band, band)
+            momentum_out[:, span] = (
+                DECAY * momentum_ref[:, span] + total[k * owned : (k + 1) * owned] * scale
+            )
     tile = 2 * owned
     index = me_r * cols + me_c
     first = pl.multiple_of(lax.div(index, 2) * tile, tile)
@@ -362,7 +383,7 @@
     sites = site_rows * site_cols
     patch = dictionary.shape[1]
     cell = patch // SPAN // SPAN
-    band, half = patch // SPAN, patch // 2
+    band = patch // SPAN
     owned = momentum.shape[0]
     rows, cols = lax.axis_size("row"), lax.axis_size("col")
     phases = SWEEPS + 1
@@ -404,15 +425,18 @@
             vmem((atoms // rows, rows * sites), BF16),
             vmem((rows, site_rows * 3 // 2, site_cols, 128), BF16),
             vmem((rows, site_rows * 6, 128), BF16),
-            vmem((cols, 2 * owned, half), BF16),
-            vmem((cols, 2 * owned, half), BF16),
+            vmem((2, cols // 2, 2, 2 * owned, band), BF16),
+            vmem((2, cols // 2, 2 * owned, band), BF16),
+            vmem((2, cols // 2, 2 * owned, band), BF16),
+            vmem((2, cols // 2, 2 * owned, band), BF16),
             vmem((owned, patch), F32),
             dma((SPAN + 2,)),
             dma((phases, 8)), dma((phases, 8)),
             dma((rows,)), dma((rows,)),
             dma((rows,)), dma((rows,)),
             dma((rows,)), dma((rows,)),
-            dma((cols,)), dma((cols,)),
+            dma((2,)), dma((2,)),
+            dma((2, cols // 2)), dma((2, cols // 2)),
         ],
         compiler_params=pltpu.CompilerParams(
             collective_id=0, has_side_effects=True, vmem_limit_bytes=48 * 2**20

time: 58 us -> 54.4 us (0.938)
  Pallas kernels: 52.3 us -> 48.7 us
    pallas_call x1, Pallas kernels: 52.3 us -> 48.7 us  [shards(): pl.pallas_call(functools.partial(kernel, rows, cols), out_shape=(jax.Shap...]
where the time goes in v4:
time: 54.4 us; the launch traced here: 54.2 us
  Pallas kernels  48.7 us (90%)
  local copies, waits for them, and re-layouts  4.89 us (9%)
  between operations  0.65 us (1%)
    pallas_call x1, Pallas kernels, shards(): pl.pallas_call(functools.partial(kernel, rows, cols), out_shape=(jax.Shap...  48.7 us
    unnamed x9, local copies, waits for them, and re-layouts  4.89 us

profile of v4, /device:TPU:1, one launch (start us, length us, event | category | flops | bytes accessed | tf_op | source)
XLA Modules:
  0.0 54.2 jit_solution(14426813110310514436)
XLA Ops:
  0.6 0.0 copy-start
  0.6 1.0 %copy-done = f32[8,16,1024]{2,1,0:T(8,128)S(1)} copy-done((f32[8,16,1024]{2,1,0:T(8,128)S(1)}, f32[8,16,1024]{2,1,0:T(8,128)}, u32[]{:S(2)}) %copy-start) | copy-done | bytes 524312
  1.7 0.0 copy-start.1
  1.7 0.9 %copy-done.1 = f32[3,64,128]{2,1,0:T(8,128)S(1)} copy-done((f32[3,64,128]{2,1,0:T(8,128)S(1)}, f32[3,64,128]{2,1,0:T(8,128)}, u32[]{:S(2)}) %copy-start.1) | copy-done | bytes 98328
  2.6 0.0 copy-start.2
  2.6 0.9 %copy-done.2 = f32[8,3072]{1,0:T(8,128)S(1)} copy-done((f32[8,3072]{1,0:T(8,128)S(1)}, f32[8,3072]{1,0:T(8,128)}, u32[]{:S(2)}) %copy-start.2) | copy-done | bytes 98328
  3.5 48.7 %shard_map.67 = (f32[128,1024]{1,0:T(8,128)S(1)}, f32[8,3072]{1,0:T(8,128)S(1)}, f32[8,3072]{1,0:T(8,128)S(1)}) custom-call(f32[3,64,128]{2,1,0:T(8,128)S(1)} %copy-done.1, f32[128,1024]{1,0:T(8,128)S(1)} %bitcast.3, bf16[1024,3072]{1,0:T(8,128)(2,1)} %dictionary_hbm.1, f32[8,3072]{1,0:T(8,128)S(1)} %copy-done.2), custom_call_target="tpu_custom_call" | custom-call | tf_op jit(solution)/shard_map/pallas_call | solution.py:393
  52.1 0.8 %copy.10 = f32[8,16,1024]{2,1,0:T(8,128)} copy(f32[8,16,1024]{2,1,0:T(8,128)S(1)} %bitcast.2) | data formatting | bytes 1048576
  52.9 0.6 %copy.11 = f32[8,3072]{1,0:T(8,128)} copy(f32[8,3072]{1,0:T(8,128)S(1)} %get-tuple-element.13) | data formatting | bytes 196608
  53.6 0.6 %copy.12 = f32[8,3072]{1,0:T(8,128)} copy(f32[8,3072]{1,0:T(8,128)S(1)} %get-tuple-element.14) | data formatting | bytes 196608
Async XLA Ops:
  0.6 1.0 %copy-start = (f32[8,16,1024]{2,1,0:T(8,128)S(1)}, f32[8,16,1024]{2,1,0:T(8,128)}, u32[]{:S(2)}) copy-start(f32[8,16,1024]{2,1,0:T(8,128)} %param.5) | copy-start | bytes 1572868
  1.7 0.9 %copy-start.1 = (f32[3,64,128]{2,1,0:T(8,128)S(1)}, f32[3,64,128]{2,1,0:T(8,128)}, u32[]{:S(2)}) copy-start(f32[3,64,128]{2,1,0:T(8,128)} %picture_ref.1) | copy-start | bytes 294916
  2.6 0.9 %copy-start.2 = (f32[8,3072]{1,0:T(8,128)S(1)}, f32[8,3072]{1,0:T(8,128)}, u32[]{:S(2)}) copy-start(f32[8,3072]{1,0:T(8,128)} %momentum_hbm.1) | copy-start | bytes 294916

commit v5 on v4

--- a/solution.py
+++ b/solution.py
@@ -68,13 +68,13 @@
 
 def kernel(
     rows, cols,
-    picture_ref, membrane_hbm, dictionary_hbm, momentum_hbm,
-    codes_out, dictionary_out, momentum_out,
+    picture_ref, membrane_hbm, dictionary_hbm,
+    codes_out, learning_out, atoms_out,
     dic, dic_t, pot, coding, cells_ref, acc, zbuf, cbuf, ext, wide,
     down_out, up_out, t_out, l_out, above_in, below_in, left_in, right_in, corner_in,
     res_ref, edge_ref,
     codes_t, strip_codes, strip_res, strip_edge, share_out, pair_in, summed, share_in,
-    momentum_ref, load_sem, spill_send, spill_recv,
+    load_sem, spill_send, spill_recv,
     code_send, code_recv, res_send, res_recv, rim_send, rim_recv,
     pair_send, pair_recv, share_send, share_recv,
 ):
@@ -85,7 +85,7 @@
     pair = band // 2
     scale = patch ** (-0.5)
     share = atoms // rows
-    owned = momentum_ref.shape[0]
+    owned = learning_out.shape[0]
     me_r, me_c = lax.axis_index("row"), lax.axis_index("col")
 
     def at(dr, dc):
@@ -106,8 +106,7 @@
         for d in range(SPAN)
     ]
     membrane_load = pltpu.make_async_copy(membrane_hbm, pot, load_sem.at[SPAN])
-    momentum_load = pltpu.make_async_copy(momentum_hbm, momentum_ref, load_sem.at[SPAN + 1])
-    for load in [membrane_load] + loads + [momentum_load]:
+    for load in [membrane_load] + loads:
         load.start()
 
     barrier = pltpu.get_barrier_semaphore()
@@ -127,6 +126,10 @@
         for copy in copies:
             copy.start()
         sent.extend(copies)
+
+    def settle(keep=0):
+        while len(sent) > keep:
+            sent.pop(0).wait_send()
 
     sub = lax.broadcasted_iota(jnp.int32, (1, 8, cell), 1)
     low = sub < 4
@@ -203,6 +206,7 @@
             pl.semaphore_wait(barrier, len(peers))
         send(copies)
         meanwhile()
+        settle(len(copies) + (rows - 1 if last else 0))
         return copies
 
     has_above, has_below = me_r > 0, me_r < rows - 1
@@ -309,6 +313,7 @@
     ]
     for j in range(rows):
         send([rim_copies[j]] + ([res_copies[j]] if j else []))
+    settle(2 * rows - 1)
     for j in range(rows):
         rim_copies[j].wait_recv()
         if j:
@@ -354,7 +359,7 @@
             for j in range(1, chips)
         ])
         send(share_copies[e])
-    momentum_load.wait()
+    settle(2 * (chips - 1))
     for e in range(2):
         total = summed[e, chip].astype(F32)
         for j in range(1, chips):
@@ -362,20 +367,28 @@
             total += share_in[e, j].astype(F32)
         for k in range(2):
             span = pl.ds((e + 2 * k) * band, band)
-            momentum_out[:, span] = (
-                DECAY * momentum_ref[:, span] + total[k * owned : (k + 1) * owned] * scale
-            )
+            learning_out[:, span] = total[k * owned : (k + 1) * owned] * scale
     tile = 2 * owned
     index = me_r * cols + me_c
     first = pl.multiple_of(lax.div(index, 2) * tile, tile)
     both = dic[pl.ds(first, tile)].astype(F32)
-    own_atoms = jnp.where(lax.rem(index, 2) == 1, both[owned:], both[:owned])
-    weights = own_atoms + LEARNING * momentum_out[...]
+    atoms_out[...] = jnp.where(lax.rem(index, 2) == 1, both[owned:], both[:owned])
+    settle()
+
+
+def finish(
+    codes_ref, learning_ref, atoms_ref, momentum_ref,
+    codes_out, dictionary_out, momentum_out, sem,
+):
+    codes_copy = pltpu.make_async_copy(codes_ref, codes_out, sem)
+    codes_copy.start()
+    momentum = DECAY * momentum_ref[...] + learning_ref[...]
+    weights = atoms_ref[...] + LEARNING * momentum
+    momentum_out[...] = momentum
     dictionary_out[...] = weights * lax.rsqrt(
         jnp.mean(weights * weights, axis=1, keepdims=True) + EPSILON
     )
-    for copy in sent:
-        copy.wait_send()
+    codes_copy.wait()
 
 
 def shards(picture, membrane, dictionary, momentum):
@@ -390,14 +403,14 @@
     vmem, dma = pltpu.VMEM, pltpu.SemaphoreType.DMA
     anywhere = pl.BlockSpec(memory_space=pltpu.HBM)
     in_vmem = pl.BlockSpec(memory_space=pltpu.VMEM)
-    codes, new_dictionary, new_momentum = pl.pallas_call(
+    results = pl.pallas_call(
         functools.partial(kernel, rows, cols),
         out_shape=(
             jax.ShapeDtypeStruct((sites, atoms), F32),
             jax.ShapeDtypeStruct((owned, patch), F32),
             jax.ShapeDtypeStruct((owned, patch), F32),
         ),
-        in_specs=[in_vmem, anywhere, anywhere, anywhere],
+        in_specs=[in_vmem, anywhere, anywhere],
         out_specs=(in_vmem, in_vmem, in_vmem),
         scratch_shapes=[
             vmem((atoms, patch), BF16),
@@ -429,8 +442,7 @@
             vmem((2, cols // 2, 2 * owned, band), BF16),
             vmem((2, cols // 2, 2 * owned, band), BF16),
             vmem((2, cols // 2, 2 * owned, band), BF16),
-            vmem((owned, patch), F32),
-            dma((SPAN + 2,)),
+            dma((SPAN + 1,)),
             dma((phases, 8)), dma((phases, 8)),
             dma((rows,)), dma((rows,)),
             dma((rows,)), dma((rows,)),
@@ -441,7 +453,15 @@
         compiler_params=pltpu.CompilerParams(
             collective_id=0, has_side_effects=True, vmem_limit_bytes=48 * 2**20
         ),
-    )(picture, membrane.reshape(sites, atoms), dictionary, momentum)
+    )(picture, membrane.reshape(sites, atoms), dictionary)
+    codes, new_dictionary, new_momentum = pl.pallas_call(
+        finish,
+        out_shape=tuple(jax.ShapeDtypeStruct(x.shape, x.dtype) for x in results),
+        in_specs=[in_vmem] * 4,
+        out_specs=(anywhere, in_vmem, in_vmem),
+        scratch_shapes=[dma(())],
+        compiler_params=pltpu.CompilerParams(vmem_limit_bytes=4 * 2**20),
+    )(*results, momentum)
     return codes.reshape(membrane.shape), new_dictionary, new_momentum
 
 

time: 54.4 us -> 53.2 us (0.978)
  local copies, waits for them, and re-layouts: 4.89 us -> 1.93 us
  Pallas kernels: 48.7 us -> 50.4 us
    unnamed x9 -> x6, local copies, waits for them, and re-layouts: 4.89 us -> 1.93 us
    pallas_call x0 -> x1, Pallas kernels: none -> 1.49 us  [shards(): pl.pallas_call(finish, out_shape=tuple((jax.ShapeDtypeStruct(x.shape, x.d...]
where the time goes in v5:
time: 53.2 us; the launch traced here: 53 us
  Pallas kernels  50.4 us (95%)
  local copies, waits for them, and re-layouts  1.93 us (4%)
  between operations  0.66 us (1%)
    pallas_call x1, Pallas kernels, shards(): pl.pallas_call(functools.partial(kernel, rows, cols), out_shape=(jax.Shap...  49 us
    unnamed x6, local copies, waits for them, and re-layouts  1.93 us
    pallas_call x1, Pallas kernels, shards(): pl.pallas_call(finish, out_shape=tuple((jax.ShapeDtypeStruct(x.shape, x.d...  1.49 us

profile of v5, /device:TPU:1, one launch (start us, length us, event | category | flops | bytes accessed | tf_op | source)
XLA Modules:
  0.0 53.0 jit_solution(15040014267443010859)
XLA Ops:
  0.6 0.0 copy-start
  0.6 1.0 %copy-done = f32[8,16,1024]{2,1,0:T(8,128)S(1)} copy-done((f32[8,16,1024]{2,1,0:T(8,128)S(1)}, f32[8,16,1024]{2,1,0:T(8,128)}, u32[]{:S(2)}) %copy-start) | copy-done | bytes 524312
  1.7 0.0 copy-start.2
  1.7 0.9 %copy-done.2 = f32[3,64,128]{2,1,0:T(8,128)S(1)} copy-done((f32[3,64,128]{2,1,0:T(8,128)S(1)}, f32[3,64,128]{2,1,0:T(8,128)}, u32[]{:S(2)}) %copy-start.2) | copy-done | bytes 98328
  2.6 0.0 copy-start.1
  2.6 49.0 %shard_map.67 = (f32[128,1024]{1,0:T(8,128)S(1)}, f32[8,3072]{1,0:T(8,128)S(1)}, f32[8,3072]{1,0:T(8,128)S(1)}) custom-call(f32[3,64,128]{2,1,0:T(8,128)S(1)} %copy-done.2, f32[128,1024]{1,0:T(8,128)S(1)} %bitcast.2, bf16[1024,3072]{1,0:T(8,128)(2,1)} %dictionary_hbm.1), custom_call_target="tpu_custom_call" | custom-call | tf_op jit(solution)/shard_map/pallas_call | solution.py:406
  51.5 0.0 copy-done.1
  51.5 1.5 %shard_map.68 = (f32[128,1024]{1,0:T(8,128)}, f32[8,3072]{1,0:T(8,128)}, f32[8,3072]{1,0:T(8,128)}) custom-call(f32[128,1024]{1,0:T(8,128)S(1)} %get-tuple-element.9.codes_ref, f32[8,3072]{1,0:T(8,128)S(1)} %get-tuple-element.10.learning_ref, f32[8,3072]{1,0:T(8,128)S(1)} %get-tuple-element.11.atoms_ref, f32[8,3072]{1,0:T(8,128)S(1)} %copy-done.1), custom_call_target="tpu_custom_call" | custom-call | tf_op jit(solution)/shard_map/pallas_call | solution.py:457
Async XLA Ops:
  0.6 1.0 %copy-start = (f32[8,16,1024]{2,1,0:T(8,128)S(1)}, f32[8,16,1024]{2,1,0:T(8,128)}, u32[]{:S(2)}) copy-start(f32[8,16,1024]{2,1,0:T(8,128)} %param.5) | copy-start | bytes 1572868
  1.7 0.9 %copy-start.2 = (f32[3,64,128]{2,1,0:T(8,128)S(1)}, f32[3,64,128]{2,1,0:T(8,128)}, u32[]{:S(2)}) copy-start(f32[3,64,128]{2,1,0:T(8,128)} %picture_ref.1) | copy-start | bytes 294916
  2.6 49.0 %copy-start.1 = (f32[8,3072]{1,0:T(8,128)S(1)}, f32[8,3072]{1,0:T(8,128)}, u32[]{:S(2)}) copy-start(f32[8,3072]{1,0:T(8,128)} %momentum_ref.1) | copy-start | bytes 294916

commit v6 on v5

--- a/solution.py
+++ b/solution.py
@@ -68,9 +68,9 @@
 
 def kernel(
     rows, cols,
-    picture_ref, membrane_hbm, dictionary_hbm,
+    picture_hbm, membrane_hbm, dictionary_hbm,
     codes_out, learning_out, atoms_out,
-    dic, dic_t, pot, coding, cells_ref, acc, zbuf, cbuf, ext, wide,
+    picture_ref, dic, dic_t, pot, coding, cells_ref, acc, zbuf, cbuf, ext, wide,
     down_out, up_out, t_out, l_out, above_in, below_in, left_in, right_in, corner_in,
     res_ref, edge_ref,
     codes_t, strip_codes, strip_res, strip_edge, share_out, pair_in, summed, share_in,
@@ -106,7 +106,8 @@
         for d in range(SPAN)
     ]
     membrane_load = pltpu.make_async_copy(membrane_hbm, pot, load_sem.at[SPAN])
-    for load in [membrane_load] + loads:
+    picture_load = pltpu.make_async_copy(picture_hbm, picture_ref, load_sem.at[SPAN + 1])
+    for load in [membrane_load] + loads[:1] + [picture_load] + loads[1:]:
         load.start()
 
     barrier = pltpu.get_barrier_semaphore()
@@ -117,7 +118,6 @@
     wide[rows * site_rows :] = jnp.zeros((MARGIN, site_cols, band), BF16)
     zbuf[...] = jnp.zeros_like(zbuf)
     cbuf[...] = jnp.zeros_like(cbuf)
-    cells_ref[...] = cells_of(picture_ref[...])
     membrane_load.wait()
     coding[...] = shrink(pot[...]).astype(BF16)
     sent = []
@@ -163,6 +163,9 @@
         cbuf[: site_rows + MARGIN] = every[:, :, :cell]
         cbuf[: site_rows + MARGIN, 1 : site_cols + 3] += every[:, : site_cols + 2, cell:]
         ext[...] = cbuf[...] * -scale
+        if phase == 0:
+            picture_load.wait()
+            cells_ref[...] = cells_of(picture_ref[...])
         ext[:site_rows, :site_cols] += cells_ref[...]
         beyond = packed(ext[:, site_cols:])
         within = packed(jnp.where(low, ext[:, :8], 0.0))
@@ -353,17 +356,18 @@
     for e in range(2):
         pair_copies[e].wait_recv()
         summed[e] = (share_out[e, :, core].astype(F32) + pair_in[e].astype(F32)).astype(BF16)
-        share_copies.append([
-            remote(summed.at[e, lax.rem(chip + j, chips)], share_in.at[e, j],
-                   share_send.at[e, j], share_recv.at[e, j], 0, 2 * j)
-            for j in range(1, chips)
-        ])
-        send(share_copies[e])
-    settle(2 * (chips - 1))
+    share_copies = [
+        remote(summed.at[:, lax.rem(chip + j, chips)], share_in.at[:, j],
+               share_send.at[0, j], share_recv.at[0, j], 0, 2 * j)
+        for j in range(1, chips)
+    ]
+    send(share_copies)
+    settle(chips - 1)
+    for copy in share_copies:
+        copy.wait_recv()
     for e in range(2):
         total = summed[e, chip].astype(F32)
         for j in range(1, chips):
-            share_copies[e][j - 1].wait_recv()
             total += share_in[e, j].astype(F32)
         for k in range(2):
             span = pl.ds((e + 2 * k) * band, band)
@@ -410,9 +414,10 @@
             jax.ShapeDtypeStruct((owned, patch), F32),
             jax.ShapeDtypeStruct((owned, patch), F32),
         ),
-        in_specs=[in_vmem, anywhere, anywhere],
+        in_specs=[anywhere, anywhere, anywhere],
         out_specs=(in_vmem, in_vmem, in_vmem),
         scratch_shapes=[
+            vmem(picture.shape, F32),
             vmem((atoms, patch), BF16),
             vmem((patch, atoms), BF16),
             vmem((sites, atoms), F32),
@@ -442,7 +447,7 @@
             vmem((2, cols // 2, 2 * owned, band), BF16),
             vmem((2, cols // 2, 2 * owned, band), BF16),
             vmem((2, cols // 2, 2 * owned, band), BF16),
-            dma((SPAN + 1,)),
+            dma((SPAN + 2,)),
             dma((phases, 8)), dma((phases, 8)),
             dma((rows,)), dma((rows,)),
             dma((rows,)), dma((rows,)),
@@ -451,7 +456,7 @@
             dma((2, cols // 2)), dma((2, cols // 2)),
         ],
         compiler_params=pltpu.CompilerParams(
-            collective_id=0, has_side_effects=True, vmem_limit_bytes=48 * 2**20
+            collective_id=0, has_side_effects=True, vmem_limit_bytes=int(53 * 2**20)
         ),
     )(picture, membrane.reshape(sites, atoms), dictionary)
     codes, new_dictionary, new_momentum = pl.pallas_call(

time: 53.2 us -> 52.5 us (0.987)
  local copies, waits for them, and re-layouts: 1.93 us -> 0.92 us
    unnamed x6 -> x4, local copies, waits for them, and re-layouts: 1.93 us -> 0.92 us
where the time goes in v6:
time: 52.5 us; the launch traced here: 52.3 us
  Pallas kernels  50.7 us (97%)
  local copies, waits for them, and re-layouts  0.92 us (2%)
  between operations  0.66 us (1%)
    pallas_call x1, Pallas kernels, shards(): pl.pallas_call(functools.partial(kernel, rows, cols), out_shape=(jax.Shap...  49.2 us
    pallas_call x1, Pallas kernels, shards(): pl.pallas_call(finish, out_shape=tuple((jax.ShapeDtypeStruct(x.shape, x.d...  1.49 us

profile of v6, /device:TPU:1, one launch (start us, length us, event | category | flops | bytes accessed | tf_op | source)
XLA Modules:
  0.0 52.3 jit_solution(3584101411909209949)
XLA Ops:
  0.6 0.0 copy-start
  0.6 0.0 copy-start.1
  0.7 0.9 %copy-done.1 = f32[3,64,128]{2,1,0:T(8,128)S(1)} copy-done((f32[3,64,128]{2,1,0:T(8,128)S(1)}, f32[3,64,128]{2,1,0:T(8,128)}, u32[]{:S(2)}) %copy-start.1) | copy-done | bytes 98328
  1.6 49.2 %shard_map.67 = (f32[128,1024]{1,0:T(8,128)S(1)}, f32[8,3072]{1,0:T(8,128)S(1)}, f32[8,3072]{1,0:T(8,128)S(1)}) custom-call(f32[3,64,128]{2,1,0:T(8,128)S(1)} %copy-done.1, f32[128,1024]{1,0:T(8,128)} %bitcast.2, bf16[1024,3072]{1,0:T(8,128)(2,1)} %dictionary_hbm.1), custom_call_target="tpu_custom_call" | custom-call | tf_op jit(solution)/shard_map/pallas_call | solution.py:410
  50.8 0.0 copy-done
  50.8 1.5 %shard_map.68 = (f32[128,1024]{1,0:T(8,128)}, f32[8,3072]{1,0:T(8,128)}, f32[8,3072]{1,0:T(8,128)}) custom-call(f32[128,1024]{1,0:T(8,128)S(1)} %get-tuple-element.9.codes_ref, f32[8,3072]{1,0:T(8,128)S(1)} %get-tuple-element.10.learning_ref, f32[8,3072]{1,0:T(8,128)S(1)} %get-tuple-element.11.atoms_ref, f32[8,3072]{1,0:T(8,128)S(1)} %copy-done), custom_call_target="tpu_custom_call" | custom-call | tf_op jit(solution)/shard_map/pallas_call | solution.py:462
Async XLA Ops:
  0.6 50.2 %copy-start = (f32[8,3072]{1,0:T(8,128)S(1)}, f32[8,3072]{1,0:T(8,128)}, u32[]{:S(2)}) copy-start(f32[8,3072]{1,0:T(8,128)} %momentum_ref.1) | copy-start | bytes 294916
  0.6 0.9 %copy-start.1 = (f32[3,64,128]{2,1,0:T(8,128)S(1)}, f32[3,64,128]{2,1,0:T(8,128)}, u32[]{:S(2)}) copy-start(f32[3,64,128]{2,1,0:T(8,128)} %picture_hbm.1) | copy-start | bytes 294916

commit v7 on v6

--- a/solution.py
+++ b/solution.py
@@ -172,42 +172,44 @@
         tight = lambda part: part.reshape(-1, cell)
         tail, head = slice(site_rows // 2, None), slice(0, 2)
         last = phase == SWEEPS
+        own_t = site_rows * 4
+        main = MARGIN * site_cols
+        corner = pl.ds(own_t, 16)
+
+        def hop(k, src, dst, dr, dc):
+            return remote(src, dst, spill_send.at[phase, k], spill_recv.at[phase, k], dr, dc)
+
+        copies = []
+
+        def go(*some):
+            send(some)
+            copies.extend(some)
+
+        if phase == 0:
+            pl.semaphore_wait(barrier, len(peers))
         t_out[phase] = tight(beyond).astype(BF16)
+        reach = own_t if last else own_t + 16
+        go(
+            hop(0, t_out.at[phase, corner], corner_in.at[phase, 0], 1, 1),
+            hop(2, t_out.at[phase, pl.ds(0, reach)], left_in.at[phase, pl.ds(0, reach)], 0, 1),
+        )
         down_out[phase] = jnp.concatenate(
             [tight(ext[site_rows : site_rows + MARGIN, :site_cols]), tight(beyond[tail])]
         ).astype(BF16)
+        reach = main if last else main + 16
+        go(hop(1, down_out.at[phase, pl.ds(0, reach)], above_in.at[phase, pl.ds(0, reach)], 1, 0))
         if not last:
             l_out[phase] = tight(within).astype(BF16)
+            go(
+                hop(3, l_out.at[phase, pl.ds(0, 16)], corner_in.at[phase, 1], -1, -1),
+                hop(4, l_out.at[phase, corner], corner_in.at[phase, 2], 1, -1),
+                hop(5, t_out.at[phase, pl.ds(0, 16)], corner_in.at[phase, 3], -1, 1),
+                hop(7, l_out.at[phase], right_in.at[phase], 0, -1),
+            )
             up_out[phase] = jnp.concatenate(
                 [tight(ext[:MARGIN, :site_cols]), tight(beyond[head])]
             ).astype(BF16)
-        own_t = site_rows * 4
-        main = MARGIN * site_cols
-        corner = pl.ds(own_t, 16)
-
-        def hop(k, src, dst, dr, dc):
-            return remote(src, dst, spill_send.at[phase, k], spill_recv.at[phase, k], dr, dc)
-
-        if last:
-            copies = [
-                hop(0, t_out.at[phase, corner], corner_in.at[phase, 0], 1, 1),
-                hop(1, down_out.at[phase, pl.ds(0, main)], above_in.at[phase, pl.ds(0, main)], 1, 0),
-                hop(2, t_out.at[phase, pl.ds(0, own_t)], left_in.at[phase, pl.ds(0, own_t)], 0, 1),
-            ]
-        else:
-            copies = [
-                hop(0, t_out.at[phase, corner], corner_in.at[phase, 0], 1, 1),
-                hop(3, l_out.at[phase, pl.ds(0, 16)], corner_in.at[phase, 1], -1, -1),
-                hop(4, l_out.at[phase, corner], corner_in.at[phase, 2], 1, -1),
-                hop(5, t_out.at[phase, pl.ds(0, 16)], corner_in.at[phase, 3], -1, 1),
-                hop(1, down_out.at[phase], above_in.at[phase], 1, 0),
-                hop(6, up_out.at[phase], below_in.at[phase], -1, 0),
-                hop(2, t_out.at[phase], left_in.at[phase], 0, 1),
-                hop(7, l_out.at[phase], right_in.at[phase], 0, -1),
-            ]
-        if phase == 0:
-            pl.semaphore_wait(barrier, len(peers))
-        send(copies)
+            go(hop(6, up_out.at[phase], below_in.at[phase], -1, 0))
         meanwhile()
         settle(len(copies) + (rows - 1 if last else 0))
         return copies

time: 52.5 us -> 52.5 us (level)
  no operation moved by 1% of the time
where the time goes in v7:
time: 52.5 us; the launch traced here: 52.3 us
  Pallas kernels  50.7 us (97%)
  local copies, waits for them, and re-layouts  0.92 us (2%)
  between operations  0.66 us (1%)
    pallas_call x1, Pallas kernels, shards(): pl.pallas_call(functools.partial(kernel, rows, cols), out_shape=(jax.Shap...  49.2 us
    pallas_call x1, Pallas kernels, shards(): pl.pallas_call(finish, out_shape=tuple((jax.ShapeDtypeStruct(x.shape, x.d...  1.49 us

profile of v7, /device:TPU:1, one launch (start us, length us, event | category | flops | bytes accessed | tf_op | source)
XLA Modules:
  0.0 52.3 jit_solution(1606287884950711363)
XLA Ops:
  0.6 0.0 copy-start
  0.6 0.0 copy-start.1
  0.7 0.9 %copy-done.1 = f32[3,64,128]{2,1,0:T(8,128)S(1)} copy-done((f32[3,64,128]{2,1,0:T(8,128)S(1)}, f32[3,64,128]{2,1,0:T(8,128)}, u32[]{:S(2)}) %copy-start.1) | copy-done | bytes 98328
  1.6 49.2 %shard_map.67 = (f32[128,1024]{1,0:T(8,128)S(1)}, f32[8,3072]{1,0:T(8,128)S(1)}, f32[8,3072]{1,0:T(8,128)S(1)}) custom-call(f32[3,64,128]{2,1,0:T(8,128)S(1)} %copy-done.1, f32[128,1024]{1,0:T(8,128)} %bitcast.2, bf16[1024,3072]{1,0:T(8,128)(2,1)} %dictionary_hbm.1), custom_call_target="tpu_custom_call" | custom-call | tf_op jit(solution)/shard_map/pallas_call | solution.py:412
  50.8 0.0 copy-done
  50.8 1.5 %shard_map.68 = (f32[128,1024]{1,0:T(8,128)}, f32[8,3072]{1,0:T(8,128)}, f32[8,3072]{1,0:T(8,128)}) custom-call(f32[128,1024]{1,0:T(8,128)S(1)} %get-tuple-element.9.codes_ref, f32[8,3072]{1,0:T(8,128)S(1)} %get-tuple-element.10.learning_ref, f32[8,3072]{1,0:T(8,128)S(1)} %get-tuple-element.11.atoms_ref, f32[8,3072]{1,0:T(8,128)S(1)} %copy-done), custom_call_target="tpu_custom_call" | custom-call | tf_op jit(solution)/shard_map/pallas_call | solution.py:464
Async XLA Ops:
  0.6 50.2 %copy-start = (f32[8,3072]{1,0:T(8,128)S(1)}, f32[8,3072]{1,0:T(8,128)}, u32[]{:S(2)}) copy-start(f32[8,3072]{1,0:T(8,128)} %momentum_ref.1) | copy-start | bytes 294916
  0.6 0.9 %copy-start.1 = (f32[3,64,128]{2,1,0:T(8,128)S(1)}, f32[3,64,128]{2,1,0:T(8,128)}, u32[]{:S(2)}) copy-start(f32[3,64,128]{2,1,0:T(8,128)} %picture_hbm.1) | copy-start | bytes 294916

commit v8 on v6

--- a/solution.py
+++ b/solution.py
@@ -347,14 +347,16 @@
         share_out[e] = jnp.concatenate(parts, axis=2).astype(BF16)
         pair_copies.append(
             pltpu.make_async_remote_copy(
-                src_ref=share_out.at[e, :, 1 - core], dst_ref=pair_in.at[e],
+                src_ref=share_out.at[:, :, 1 - core], dst_ref=pair_in,
                 send_sem=pair_send.at[e], recv_sem=pair_recv.at[e],
                 device_id=twin, device_id_type=MESH,
             )
         )
-        send(pair_copies[e:])
+        if e == 1:
+            send(pair_copies[1:])
     for e in range(2):
-        pair_copies[e].wait_recv()
+        if e == 0:
+            pair_copies[1].wait_recv()
         summed[e] = (share_out[e, :, core].astype(F32) + pair_in[e].astype(F32)).astype(BF16)
     share_copies = [
         remote(summed.at[:, lax.rem(chip + j, chips)], share_in.at[:, j],

time: 52.5 us -> 52.6 us (level)
  no operation moved by 1% of the time
where the time goes in v8:
time: 52.6 us; the launch traced here: 52.5 us
  Pallas kernels  50.9 us (97%)
  local copies, waits for them, and re-layouts  0.92 us (2%)
  between operations  0.66 us (1%)
    pallas_call x1, Pallas kernels, shards(): pl.pallas_call(functools.partial(kernel, rows, cols), out_shape=(jax.Shap...  49.4 us
    pallas_call x1, Pallas kernels, shards(): pl.pallas_call(finish, out_shape=tuple((jax.ShapeDtypeStruct(x.shape, x.d...  1.49 us

profile of v8, /device:TPU:1, one launch (start us, length us, event | category | flops | bytes accessed | tf_op | source)
XLA Modules:
  0.0 52.5 jit_solution(2266767842103785775)
XLA Ops:
  0.6 0.0 copy-start
  0.6 0.0 copy-start.1
  0.7 0.9 %copy-done.1 = f32[3,64,128]{2,1,0:T(8,128)S(1)} copy-done((f32[3,64,128]{2,1,0:T(8,128)S(1)}, f32[3,64,128]{2,1,0:T(8,128)}, u32[]{:S(2)}) %copy-start.1) | copy-done | bytes 98328
  1.6 49.4 %shard_map.67 = (f32[128,1024]{1,0:T(8,128)S(1)}, f32[8,3072]{1,0:T(8,128)S(1)}, f32[8,3072]{1,0:T(8,128)S(1)}) custom-call(f32[3,64,128]{2,1,0:T(8,128)S(1)} %copy-done.1, f32[128,1024]{1,0:T(8,128)} %bitcast.2, bf16[1024,3072]{1,0:T(8,128)(2,1)} %dictionary_hbm.1), custom_call_target="tpu_custom_call" | custom-call | tf_op jit(solution)/shard_map/pallas_call | solution.py:412
  51.0 0.0 copy-done
  51.0 1.5 %shard_map.68 = (f32[128,1024]{1,0:T(8,128)}, f32[8,3072]{1,0:T(8,128)}, f32[8,3072]{1,0:T(8,128)}) custom-call(f32[128,1024]{1,0:T(8,128)S(1)} %get-tuple-element.9.codes_ref, f32[8,3072]{1,0:T(8,128)S(1)} %get-tuple-element.10.learning_ref, f32[8,3072]{1,0:T(8,128)S(1)} %get-tuple-element.11.atoms_ref, f32[8,3072]{1,0:T(8,128)S(1)} %copy-done), custom_call_target="tpu_custom_call" | custom-call | tf_op jit(solution)/shard_map/pallas_call | solution.py:464
Async XLA Ops:
  0.6 50.4 %copy-start = (f32[8,3072]{1,0:T(8,128)S(1)}, f32[8,3072]{1,0:T(8,128)}, u32[]{:S(2)}) copy-start(f32[8,3072]{1,0:T(8,128)} %momentum_ref.1) | copy-start | bytes 294916
  0.6 0.9 %copy-start.1 = (f32[3,64,128]{2,1,0:T(8,128)S(1)}, f32[3,64,128]{2,1,0:T(8,128)}, u32[]{:S(2)}) copy-start(f32[3,64,128]{2,1,0:T(8,128)} %picture_hbm.1) | copy-start | bytes 294916
